TPU v7x, 32 devices: a whole 2x2x4 slice. The times are simulated.
32 devices in a mesh: seq: 2 (over y), ctx: 4 (over x, core), exp: 4 (over z).
Axes of the slice: x: 2, y: 2, z: 4, core: 2. Of those that a mesh axis runs over, the one named last changes fastest.
Arguments:
- tokens: bfloat16 [8, 1024, 768], P(('seq', 'exp'), 'ctx'), may hold values from -6 to 6
- expert_ids: int32 [8, 1024, 2], P(('seq', 'exp'), 'ctx'), may hold values from 0 to 3, all different within a row; in each aligned block of 256 rows (0 to 255, 256 to 511, ..., all dimensions but the last counted through in order) at most 256 rows name the same one
- norm_one: float32 [768], replicated, may hold values from 0.5 to 1.5
- w_query: bfloat16 [768, 768], replicated, may hold values from -0.21875 to 0.21875
- w_key: bfloat16 [768, 768], replicated, may hold values from -0.21875 to 0.21875
- w_value: bfloat16 [768, 768], replicated, may hold values from -0.21875 to 0.21875
- w_out: bfloat16 [768, 768], replicated, may hold values from -1.75 to 1.75
- norm_two: float32 [768], replicated, may hold values from 0.5 to 1.5
- w_router: bfloat16 [768, 4], replicated, may hold values from -0.21875 to 0.21875
- expert_gate: bfloat16 [4, 768, 2048], P('exp'), may hold values from -0.21875 to 0.21875
- expert_up: bfloat16 [4, 768, 2048], P('exp'), may hold values from -0.21875 to 0.21875
- expert_down: bfloat16 [4, 2048, 768], P('exp'), may hold values from -0.125 to 0.125
- shared_gate: bfloat16 [768, 2048], replicated, may hold values from -0.21875 to 0.21875
- shared_up: bfloat16 [768, 2048], replicated, may hold values from -0.21875 to 0.21875
- shared_down: bfloat16 [2048, 768], replicated, may hold values from -0.125 to 0.125
- cotangent: bfloat16 [8, 1024, 768], P(('seq', 'exp'), 'ctx'), may hold values from -6 to 6
Outputs:
- output: bfloat16 [8, 1024, 768], P(('seq', 'exp'), 'ctx')
- grad_tokens: float32 [8, 1024, 768], P(('seq', 'exp'), 'ctx')
- grad_norm_one: float32 [768], replicated
- grad_query: float32 [768, 768], P(('seq', 'ctx'), 'exp')
- grad_key: float32 [768, 768], P(('seq', 'ctx'), 'exp')
- grad_value: float32 [768, 768], P(('seq', 'ctx'), 'exp')
- grad_out: float32 [768, 768], P(('seq', 'ctx'), 'exp')
- grad_norm_two: float32 [768], replicated
- grad_router: float32 [768, 4], P(('seq', 'ctx'), 'exp')
- grad_expert_gate: float32 [4, 768, 2048], P('exp')
- grad_expert_up: float32 [4, 768, 2048], P('exp')
- grad_expert_down: float32 [4, 2048, 768], P('exp')
- grad_shared_gate: float32 [768, 2048], P(('seq', 'ctx'), 'exp')
- grad_shared_up: float32 [768, 2048], P(('seq', 'ctx'), 'exp')
- grad_shared_down: float32 [2048, 768], P(('seq', 'ctx'), 'exp')
Inputs may be any that keep to these rules, and one draw needn't show every extreme that they name: `expert_ids`: each token names 2 different experts; the tokens of one device name no expert more than 256 times, and on some device some expert is named exactly 256 times.
All inputs are finite; a program needn't handle non-finite values.
Results may differ from a plain program's by a relative error of at most 0.024.
Values may be sent and summed in bfloat16 or wider, within the bound.
A program may use at most 192 MiB of HBM per device.

v0:
```python
import math

import jax
import jax.numpy as jnp
from jax import lax
from jax.sharding import PartitionSpec as P

HEAD_DIM = 64
TOP = 2
BLOCK = 256
KEY_ROWS = 512


def product(first_factor, second_factor):
    return jnp.dot(first_factor, second_factor, preferred_element_type=jnp.float32)


def against(first_factor, second_factor):
    return lax.dot_general(
        first_factor, second_factor, (((1,), (1,)), ((), ())), preferred_element_type=jnp.float32
    )


def outer_sum(first_factor, second_factor):
    return lax.dot_general(
        first_factor, second_factor, (((0,), (0,)), ((), ())), preferred_element_type=jnp.float32
    )


def normalize(values, scaling):
    return values * lax.rsqrt(jnp.mean(values * values, axis=-1, keepdims=True) + 1e-06) * scaling


def rotate(values, places):
    halfway = values.shape[-1] // 2
    frequency = 10000.0 ** (-jnp.arange(halfway, dtype=jnp.float32) / halfway)
    angles = places.astype(jnp.float32)[:, None] * frequency[None, :]
    cosine = jnp.cos(angles)[:, None, :]
    sine_part = jnp.sin(angles)[:, None, :]
    former = values[..., :halfway]
    latter = values[..., halfway:]
    return jnp.concatenate(
        [former * cosine - latter * sine_part, latter * cosine + former * sine_part], axis=-1
    )


def silu_parts(gate_pre):
    sigmoid_value = jax.nn.sigmoid(gate_pre)
    return (gate_pre * sigmoid_value, sigmoid_value * (1.0 + gate_pre * (1.0 - sigmoid_value)))


def tiled(matrix, row_groups, col_groups):
    row_count, col_count = matrix.shape
    blocks = matrix.reshape(
        row_groups, row_count // row_groups, col_groups, col_count // col_groups
    ).transpose(0, 2, 1, 3)
    return blocks.reshape(col_groups * row_count, col_count // col_groups)


def per_device(
    tokens,
    expert_ids,
    norm_one,
    w_query,
    w_key,
    w_value,
    w_out,
    norm_two,
    w_router,
    expert_gate,
    expert_up,
    expert_down,
    shared_gate,
    shared_up,
    shared_down,
    cotangent,
):
    local_rows = tokens.shape[1]
    model_width = tokens.shape[2]
    head_count = model_width // HEAD_DIM
    score_scale = HEAD_DIM ** (-0.5)
    ctx_count = lax.axis_size("ctx")
    ctx_place = lax.axis_index("ctx")
    exp_count = lax.axis_size("exp")
    row_groups = lax.axis_size("seq") * ctx_count
    local_experts = expert_gate.shape[0]
    experts_all = local_experts * exp_count
    capacity = min(local_rows, 2 * TOP * local_rows // experts_all)
    places = ctx_place * local_rows + jnp.arange(local_rows, dtype=jnp.int32)
    query_blocks = places // BLOCK

    def spread(matrix):
        return tiled(matrix, row_groups, exp_count)

    inputs = tokens[0].astype(jnp.float32)
    normed_full, norm_one_pull = jax.vjp(normalize, inputs, norm_one)
    normed = normed_full.astype(jnp.bfloat16)
    query = rotate(
        product(normed, w_query).reshape(local_rows, head_count, HEAD_DIM), places
    ).astype(jnp.bfloat16)
    keys_local = (
        rotate(product(normed, w_key).reshape(local_rows, head_count, HEAD_DIM), places)
        .astype(jnp.bfloat16)
        .reshape(local_rows, model_width)
    )
    values_local = product(normed, w_value).astype(jnp.bfloat16)

    def block_scores(key_block, offset):
        key_heads = key_block.reshape(-1, head_count, HEAD_DIM)
        scores = (
            jnp.einsum("qhd,khd->hqk", query, key_heads, preferred_element_type=jnp.float32)
            * score_scale
        )
        key_index = (offset + jnp.arange(key_block.shape[0], dtype=jnp.int32)) // BLOCK
        allowed = key_index[None, :] <= query_blocks[:, None]
        return (scores, allowed)

    def attend_block(running, key_block, value_block, offset):
        highest, totals, accumulated = running
        scores, allowed = block_scores(key_block, offset)
        masked = jnp.where(allowed[None], scores, -1e30)
        fresh = jnp.maximum(highest, jnp.max(masked, axis=-1))
        weights = jnp.where(allowed[None], jnp.exp(masked - fresh[..., None]), 0.0)
        decay = jnp.exp(highest - fresh)
        value_heads = value_block.reshape(-1, head_count, HEAD_DIM)
        accumulated = accumulated * decay[..., None] + jnp.einsum(
            "hqk,khd->hqd",
            weights.astype(jnp.bfloat16),
            value_heads,
            preferred_element_type=jnp.float32,
        )
        return (fresh, totals * decay + jnp.sum(weights, axis=-1), accumulated)

    start_state = (
        jnp.full((head_count, local_rows), -1e30, jnp.float32),
        jnp.zeros((head_count, local_rows), jnp.float32),
        jnp.zeros((head_count, local_rows, HEAD_DIM), jnp.float32),
    )
    running = start_state
    key_part = lax.all_gather(keys_local, "ctx", axis=0, tiled=True)
    value_part = lax.all_gather(values_local, "ctx", axis=0, tiled=True)
    span_rows = key_part.shape[0]
    stride = math.gcd(span_rows, KEY_ROWS)
    step_count = span_rows // stride
    key_steps = key_part.reshape(step_count, stride, model_width)
    value_steps = value_part.reshape(step_count, stride, model_width)
    offsets = jnp.arange(step_count, dtype=jnp.int32) * stride

    def one_step(inner, operands):
        return (attend_block(inner, operands[0], operands[1], operands[2]), None)

    running, unused = lax.scan(one_step, running, (key_steps, value_steps, offsets))
    highest, totals, accumulated = running
    log_total = highest + jnp.log(totals)
    attended = (
        (accumulated / totals[..., None])
        .transpose(1, 0, 2)
        .reshape(local_rows, model_width)
        .astype(jnp.bfloat16)
    )
    mixed = inputs + product(attended, w_out)
    second_full, norm_two_pull = jax.vjp(normalize, mixed, norm_two)
    second = second_full.astype(jnp.bfloat16)
    logits = product(second, w_router)
    chosen = expert_ids[0]
    one_hot = (
        chosen[:, :, None] == jnp.arange(experts_all, dtype=jnp.int32)[None, None, :]
    ).astype(jnp.float32)
    selected = jnp.sum(logits[:, None, :] * one_hot, axis=-1)
    gates = jax.nn.softmax(selected, axis=-1)
    flat_ids = chosen.reshape(-1)
    slot_hits = (flat_ids[:, None] == jnp.arange(experts_all, dtype=jnp.int32)[None, :]).astype(
        jnp.int32
    )
    slot_place = jnp.sum((jnp.cumsum(slot_hits, axis=0) - slot_hits) * slot_hits, axis=1)

    def to_slots(routed_rows):
        empty_slots = jnp.zeros((experts_all, capacity, model_width), jnp.bfloat16)
        return (
            empty_slots.at[flat_ids, slot_place]
            .set(routed_rows)
            .reshape(exp_count, local_experts, capacity, model_width)
        )

    def from_slots(arrived_back):
        picked = arrived_back.reshape(experts_all, capacity, model_width)[flat_ids, slot_place]
        return picked.astype(jnp.float32).reshape(local_rows, TOP, model_width)

    def expert_front(arrived_rows):
        gate_pre = jnp.einsum(
            "sjcd,jdf->sjcf", arrived_rows, expert_gate, preferred_element_type=jnp.float32
        )
        up_pre = jnp.einsum(
            "sjcd,jdf->sjcf", arrived_rows, expert_up, preferred_element_type=jnp.float32
        )
        hidden = (jax.nn.silu(gate_pre) * up_pre).astype(jnp.bfloat16)
        return (gate_pre, up_pre, hidden)

    send_rows = to_slots(jnp.repeat(second, TOP, axis=0))
    arrived = lax.all_to_all(send_rows, "exp", split_axis=0, concat_axis=0, tiled=True)
    gate_pre, up_pre, hidden = expert_front(arrived)
    results = jnp.einsum(
        "sjcf,jfd->sjcd", hidden, expert_down, preferred_element_type=jnp.float32
    ).astype(jnp.bfloat16)
    returned = lax.all_to_all(results, "exp", split_axis=0, concat_axis=0, tiled=True)
    expert_out = from_slots(returned)
    mixture = jnp.sum(gates[:, :, None] * expert_out, axis=1)
    shared_gate_pre = product(second, shared_gate)
    shared_up_pre = product(second, shared_up)
    shared_hidden = (jax.nn.silu(shared_gate_pre) * shared_up_pre).astype(jnp.bfloat16)
    output = (mixed + mixture + product(shared_hidden, shared_down)).astype(jnp.bfloat16)
    upstream = cotangent[0]
    upstream_full = upstream.astype(jnp.float32)
    grad_shared_down = outer_sum(shared_hidden, upstream)
    d_shared_hidden = against(upstream, shared_down)
    shared_silu, shared_slope = silu_parts(shared_gate_pre)
    d_shared_gate = (d_shared_hidden * shared_up_pre * shared_slope).astype(jnp.bfloat16)
    d_shared_up = (d_shared_hidden * shared_silu).astype(jnp.bfloat16)
    grad_shared_gate = outer_sum(second, d_shared_gate)
    grad_shared_up = outer_sum(second, d_shared_up)
    d_second = against(d_shared_gate, shared_gate) + against(d_shared_up, shared_up)
    d_gates = jnp.sum(upstream_full[:, None, :] * expert_out, axis=-1)
    d_selected = gates * (d_gates - jnp.sum(gates * d_gates, axis=-1, keepdims=True))
    d_logits = jnp.sum(d_selected[:, :, None] * one_hot, axis=1).astype(jnp.bfloat16)
    grad_router = outer_sum(second, d_logits)
    d_second = d_second + against(d_logits, w_router)
    grad_slots = to_slots(
        (gates[:, :, None] * upstream_full[:, None, :])
        .astype(jnp.bfloat16)
        .reshape(local_rows * TOP, model_width)
    )
    arrived_rows, arrived_grad = (
        lax.all_to_all(send_rows, "exp", split_axis=0, concat_axis=0, tiled=True),
        lax.all_to_all(grad_slots, "exp", split_axis=0, concat_axis=0, tiled=True),
    )
    gate_kept, up_kept, hidden_kept = expert_front(arrived_rows)
    d_hidden = jnp.einsum(
        "sjcd,jfd->sjcf", arrived_grad, expert_down, preferred_element_type=jnp.float32
    )
    expert_silu, expert_slope = silu_parts(gate_kept)
    d_gate_pre = (d_hidden * up_kept * expert_slope).astype(jnp.bfloat16)
    d_up_pre = (d_hidden * expert_silu).astype(jnp.bfloat16)
    grad_expert_down = jnp.einsum(
        "sjcf,sjcd->jfd", hidden_kept, arrived_grad, preferred_element_type=jnp.float32
    )
    grad_expert_gate = jnp.einsum(
        "sjcd,sjcf->jdf", arrived_rows, d_gate_pre, preferred_element_type=jnp.float32
    )
    grad_expert_up = jnp.einsum(
        "sjcd,sjcf->jdf", arrived_rows, d_up_pre, preferred_element_type=jnp.float32
    )
    d_routed = (
        jnp.einsum("sjcf,jdf->sjcd", d_gate_pre, expert_gate, preferred_element_type=jnp.float32)
        + jnp.einsum("sjcf,jdf->sjcd", d_up_pre, expert_up, preferred_element_type=jnp.float32)
    ).astype(jnp.bfloat16)
    returned_grad = lax.all_to_all(d_routed, "exp", split_axis=0, concat_axis=0, tiled=True)
    d_second = d_second + jnp.sum(from_slots(returned_grad), axis=1)
    grad_expert_gate, grad_expert_up, grad_expert_down = (
        lax.psum(grad_expert_gate.astype(jnp.bfloat16), ("seq", "ctx")).astype(jnp.float32),
        lax.psum(grad_expert_up.astype(jnp.bfloat16), ("seq", "ctx")).astype(jnp.float32),
        lax.psum(grad_expert_down.astype(jnp.bfloat16), ("seq", "ctx")).astype(jnp.float32),
    )
    d_mixed_part, grad_norm_two = norm_two_pull(d_second)
    d_mixed = upstream_full + d_mixed_part
    d_attention = d_mixed.astype(jnp.bfloat16)
    grad_out = outer_sum(attended, d_attention)
    grad_heads = (
        against(d_attention, w_out).astype(jnp.bfloat16).reshape(local_rows, head_count, HEAD_DIM)
    )
    keys_all, values_all = (
        lax.all_gather(keys_local, "ctx", axis=0, tiled=True),
        lax.all_gather(values_local, "ctx", axis=0, tiled=True),
    )
    block_total = ((ctx_place + 1) * local_rows + KEY_ROWS - 1) // KEY_ROWS

    def weights_at(number):
        offset = number * KEY_ROWS
        key_block = lax.dynamic_slice_in_dim(keys_all, offset, KEY_ROWS, 0)
        value_block = lax.dynamic_slice_in_dim(values_all, offset, KEY_ROWS, 0)
        scores, allowed = block_scores(key_block, offset)
        weights = jnp.where(allowed[None], jnp.exp(scores - log_total[..., None]), 0.0)
        grad_weights = jnp.einsum(
            "qhd,khd->hqk",
            grad_heads,
            value_block.reshape(KEY_ROWS, head_count, HEAD_DIM),
            preferred_element_type=jnp.float32,
        )
        return (key_block, weights, grad_weights)

    def row_dot_step(number, summed):
        unused_block, weights, grad_weights = weights_at(number)
        return summed + jnp.sum(weights * grad_weights, axis=-1)

    row_dots = lax.fori_loop(
        0, block_total, row_dot_step, jnp.zeros((head_count, local_rows), jnp.float32)
    )

    def score_grads(number):
        key_block, weights, grad_weights = weights_at(number)
        d_scores = (weights * (grad_weights - row_dots[..., None])).astype(jnp.bfloat16)
        return (key_block.reshape(KEY_ROWS, head_count, HEAD_DIM), weights, d_scores)

    query_start = jnp.zeros((local_rows, head_count, HEAD_DIM), jnp.float32)

    def grad_step(number, running):
        grad_query, key_terms = running
        key_heads, weights, d_scores = score_grads(number)
        grad_query = (
            grad_query
            + jnp.einsum("hqk,khd->qhd", d_scores, key_heads, preferred_element_type=jnp.float32)
            * score_scale
        )
        key_part = (
            jnp.einsum("hqk,qhd->khd", d_scores, query, preferred_element_type=jnp.float32)
            * score_scale
        )
        value_part = jnp.einsum(
            "hqk,qhd->khd",
            weights.astype(jnp.bfloat16),
            grad_heads,
            preferred_element_type=jnp.float32,
        )
        block_terms = jnp.concatenate(
            [key_part.reshape(KEY_ROWS, model_width), value_part.reshape(KEY_ROWS, model_width)],
            axis=1,
        )
        return (
            grad_query,
            lax.dynamic_update_slice_in_dim(key_terms, block_terms, number * KEY_ROWS, 0),
        )

    grad_query_heads, key_terms = lax.fori_loop(
        0,
        block_total,
        grad_step,
        (query_start, jnp.zeros((ctx_count * local_rows, 2 * model_width), jnp.float32)),
    )
    key_grads = lax.psum_scatter(
        key_terms.astype(jnp.bfloat16), "ctx", scatter_dimension=0, tiled=True
    ).astype(jnp.float32)
    key_grad_heads = key_grads[:, :model_width].reshape(local_rows, head_count, HEAD_DIM)
    d_value = key_grads[:, model_width:].astype(jnp.bfloat16)
    d_query_lin = (
        rotate(grad_query_heads, -places).astype(jnp.bfloat16).reshape(local_rows, model_width)
    )
    d_key_lin = (
        rotate(key_grad_heads, -places).astype(jnp.bfloat16).reshape(local_rows, model_width)
    )
    grad_query = outer_sum(normed, d_query_lin)
    grad_key = outer_sum(normed, d_key_lin)
    grad_value = outer_sum(normed, d_value)
    d_normed = against(d_query_lin, w_query) + against(d_key_lin, w_key) + against(d_value, w_value)
    d_inputs, grad_norm_one = norm_one_pull(d_normed)
    grad_tokens = (d_mixed + d_inputs)[None]
    (
        grad_query,
        grad_key,
        grad_value,
        grad_out,
        grad_router,
        grad_shared_gate,
        grad_shared_up,
        grad_shared_down,
    ) = (
        lax.psum_scatter(
            spread(grad_query), ("seq", "ctx", "exp"), scatter_dimension=0, tiled=True
        ),
        lax.psum_scatter(spread(grad_key), ("seq", "ctx", "exp"), scatter_dimension=0, tiled=True),
        lax.psum_scatter(
            spread(grad_value), ("seq", "ctx", "exp"), scatter_dimension=0, tiled=True
        ),
        lax.psum_scatter(spread(grad_out), ("seq", "ctx", "exp"), scatter_dimension=0, tiled=True),
        lax.psum_scatter(
            spread(grad_router), ("seq", "ctx", "exp"), scatter_dimension=0, tiled=True
        ),
        lax.psum_scatter(
            spread(grad_shared_gate), ("seq", "ctx", "exp"), scatter_dimension=0, tiled=True
        ),
        lax.psum_scatter(
            spread(grad_shared_up), ("seq", "ctx", "exp"), scatter_dimension=0, tiled=True
        ),
        lax.psum_scatter(
            spread(grad_shared_down), ("seq", "ctx", "exp"), scatter_dimension=0, tiled=True
        ),
    )
    grad_norm_one, grad_norm_two = lax.psum((grad_norm_one, grad_norm_two), ("seq", "ctx", "exp"))
    return (
        output[None],
        grad_tokens,
        grad_norm_one,
        grad_query,
        grad_key,
        grad_value,
        grad_out,
        grad_norm_two,
        grad_router,
        grad_expert_gate,
        grad_expert_up,
        grad_expert_down,
        grad_shared_gate,
        grad_shared_up,
        grad_shared_down,
    )


def solution(mesh):
    in_specs = (
        P(("seq", "exp"), "ctx", None),
        P(("seq", "exp"), "ctx", None),
        P(),
        P(),
        P(),
        P(),
        P(),
        P(),
        P(),
        P("exp", None, None),
        P("exp", None, None),
        P("exp", None, None),
        P(),
        P(),
        P(),
        P(("seq", "exp"), "ctx", None),
    )
    out_specs = (
        P(("seq", "exp"), "ctx", None),
        P(("seq", "exp"), "ctx", None),
        P(),
        P(("seq", "ctx"), "exp"),
        P(("seq", "ctx"), "exp"),
        P(("seq", "ctx"), "exp"),
        P(("seq", "ctx"), "exp"),
        P(),
        P(("seq", "ctx"), "exp"),
        P("exp", None, None),
        P("exp", None, None),
        P("exp", None, None),
        P(("seq", "ctx"), "exp"),
        P(("seq", "ctx"), "exp"),
        P(("seq", "ctx"), "exp"),
    )
    return jax.shard_map(
        per_device, mesh=mesh, in_specs=in_specs, out_specs=out_specs, check_vma=False
    )
```

profile of v0, /device:TPU:0, one launch (start us, length us, event | category | flops | bytes accessed | tf_op | source)
XLA Modules:
  0.0 1572.7 jit_solution(3306183299281106826)
XLA Ops:
  34.9 9.1 all-gather.3.cloned.1.call-done
  44.0 21.8 %all-gather.5.cloned.1.call-done = bf16[1024,768]{1,0:T(8,128)(2,1)} async-done(((bf16[256,768]{1,0:T(8,128)(2,1)}), bf16[1024,768]{1,0:T(8,128)(2,1)}) %all-gather.5.cloned.1.call-update) | async-done | bytes 1572880 | tf_op jit(solution)/shard_map/all_gather | solution.py:141
  65.8 53.6 %while.47 = (s32[]{:T(128)}, f32[12,256]{1,0:T(8,128)}, f32[12,256]{1,0:T(8,128)}, f32[12,256,64]{1,2,0:T(8,128)}, s32[2]{0:T(128)S(1)}, /*index=5*/bf16[2,512,7...) while((s32[]{:T(128)}, f32[12,256]{1,0:T(8,128)}, ...), condition=%wide.region_4.5_spmd.clone, body=%wide.region_1.4_spmd.clone.sunk | while | flops 423848960 | bytes 29628680 | solution.py:152
  134.0 71.7 %scatter_fusion.1 = bf16[4,256,768]{2,1,0:T(8,128)(2,1)} fusion(bf16[4,256,768]{2,1,0:T(8,128)(2,1)} %broadcast.607.clone, s32[512]{0:T(512)S(1)} %bitcast.514, bf16[512,768]{1,0:T(8,128)(2,1)} %multiply_convert_fusion.3), kind=kCustom, calls=%fused_computation.3 | custom fusion | bytes 2363392 | tf_op jit(solution)/shard_map/scatter | solution.py:181
  219.8 71.7 %scatter_fusion = bf16[4,256,768]{2,1,0:T(8,128)(2,1)} fusion(bf16[4,256,768]{2,1,0:T(8,128)(2,1)} %broadcast.607.clone.1, s32[512]{0:T(512)S(1)} %bitcast.515, bf16[512,768]{1,0:T(8,128)(2,1)} %reshape.773), kind=kCustom, calls=%fused_computation.2 | custom fusion | bytes 2363392 | tf_op jit(solution)/shard_map/scatter | solution.py:181
  304.3 9.1 fusion.58
  313.4 22.8 %all-to-all-done = bf16[4,1,256,768]{3,2,1,0:T(8,128)(2,1)} async-done(((bf16[4,1,256,768]{3,2,1,0:T(8,128)(2,1)}), bf16[4,1,256,768]{3,2,1,0:T(8,128)(2,1)}, u32[]{:S(2)}, u32[]{:S(2)}) %all-to-all-start) | async-done | bytes 1572896 | tf_op jit(solution)/shard_map/all_to_all | solution.py:200
  336.2 9.2 fusion.64
  345.4 12.7 fusion.51
  383.4 22.6 %all-to-all-done.1 = bf16[4,1,256,768]{3,2,1,0:T(8,128)(2,1)} async-done(((bf16[4,1,256,768]{3,2,1,0:T(8,128)(2,1)}), bf16[4,1,256,768]{3,2,1,0:T(8,128)(2,1)}, u32[]{:S(2)}, u32[]{:S(2)}) %all-to-all-start.1) | async-done | bytes 1572896 | tf_op jit(solution)/shard_map/all_to_all | solution.py:205
  435.8 10.2 all-to-all-done.3
  469.9 10.5 while.46
  514.9 8.4 reshape.749
  535.6 8.4 reshape.751
  590.9 42.7 %reduce-scatter.28.cloned.1.call-done = f32[96,1]{1,0:T(8,128)} async-done(((f32[3072,1]{1,0:T(8,128)}), f32[96,1]{1,0:T(8,128)}) %reduce-scatter.28.cloned.1.call-update) | async-done | bytes 400
  635.0 140.6 %all-reduce.4.cloned.1.call-done = (bf16[1,768,2048]{2,1,0:T(8,128)(2,1)}, bf16[1,768,2048]{2,1,0:T(8,128)(2,1)}, bf16[1,2048,768]{2,1,0:T(8,128)(2,1)}) async-done(((bf16[1,768,2048]{2,1,0:T(8,128)(2,1)}, bf16[1,768,2048]{2,1,0:T(8,128)(2,1)}, bf16[1,2048,768]{2,1,0:T(8,128)(2,1)}), (bf16[1,768,2048]{2,1,0:T(8,128)(2,1)}, bf16[1,768,2048]{2,1,0:T(8,128)(2,1)}, ...) | async-done | bytes 9437200 | tf_op jit(solution)/shard_map/psum | solution.py:259
  788.0 39.5 %all-reduce = (f32[768]{0:T(1024)}, f32[768]{0:T(1024)}) all-reduce(f32[768]{0:T(1024)S(1)} %get-tuple-element.626, f32[768]{0:T(1024)S(1)} %copy-done.53), channel_id=1, replica_groups=mesh['seq'=2,'ctx'=4,'exp'=4] {'seq','ctx','exp'}, use_global_device_ids=true, to_apply=%region_28.29 | all-reduce | flops 1536 | bytes 12288 | tf_op jit(solution)/shard_map/psum | solution.py:386
  827.5 55.7 %reduce-scatter.20.cloned.1.call-done = f32[96,192]{1,0:T(8,128)} async-done(((f32[3072,192]{1,0:T(8,128)}), f32[96,192]{1,0:T(8,128)}) %reduce-scatter.20.cloned.1.call-update) | async-done | bytes 73744 | tf_op jit(solution)/shard_map/reduce_scatter | solution.py:372
  883.1 119.5 %reduce-scatter.22.cloned.1.call-done = f32[96,512]{1,0:T(8,128)} async-done(((f32[3072,512]{1,0:T(8,128)}), f32[96,512]{1,0:T(8,128)}) %reduce-scatter.22.cloned.1.call-update) | async-done | bytes 196624 | tf_op jit(solution)/shard_map/reduce_scatter | solution.py:376
  1002.7 120.7 %reduce-scatter.24.cloned.1.call-done = f32[96,512]{1,0:T(8,128)} async-done(((f32[3072,512]{1,0:T(8,128)}), f32[96,512]{1,0:T(8,128)}) %reduce-scatter.24.cloned.1.call-update) | async-done | bytes 196624 | tf_op jit(solution)/shard_map/reduce_scatter | solution.py:379
  1123.3 120.1 %reduce-scatter.26.cloned.1.call-done = f32[256,192]{0,1:T(8,128)} async-done(((f32[8192,192]{0,1:T(8,128)}), f32[256,192]{0,1:T(8,128)}) %reduce-scatter.26.cloned.1.call-update) | async-done | bytes 196624 | tf_op jit(solution)/shard_map/reduce_scatter | solution.py:382
  1243.4 107.6 %reduce-scatter.14.cloned.1.call-done = f32[96,192]{1,0:T(8,128)} async-done(((f32[3072,192]{1,0:T(8,128)}), f32[96,192]{1,0:T(8,128)}) %reduce-scatter.14.cloned.1.call-update) | async-done | bytes 73744 | tf_op jit(solution)/shard_map/reduce_scatter | solution.py:365
  1351.0 107.4 %reduce-scatter.16.cloned.1.call-done = f32[96,192]{1,0:T(8,128)} async-done(((f32[3072,192]{1,0:T(8,128)}), f32[96,192]{1,0:T(8,128)}) %reduce-scatter.16.cloned.1.call-update) | async-done | bytes 73744 | tf_op jit(solution)/shard_map/reduce_scatter | solution.py:368
  1458.4 107.3 %reduce-scatter.18.cloned.1.call-done = f32[96,192]{1,0:T(8,128)} async-done(((f32[3072,192]{1,0:T(8,128)}), f32[96,192]{1,0:T(8,128)}) %reduce-scatter.18.cloned.1.call-update) | async-done | bytes 73744 | tf_op jit(solution)/shard_map/reduce_scatter | solution.py:369
  (338 shorter events, 322.8 us)
Async XLA Ops:
  7.2 338.2 %copy-start = (bf16[1,768,2048]{2,1,0:T(8,128)(2,1)S(1)}, bf16[1,768,2048]{2,1,0:T(8,128)(2,1)}, u32[]{:S(2)}) copy-start(bf16[1,768,2048]{2,1,0:T(8,128)(2,1)} %param.31) | copy-start | bytes 9437188
  7.2 36.8 %all-gather.3.cloned.1.call-start = ((), (), s32[]{:S(2)}) async-start(), calls=%async_computation.13 | async-start | bytes 1966080 | tf_op jit(solution)/shard_map/all_gather | solution.py:140
  11.9 10.2 copy-start.46
  21.5 44.3 %all-gather.5.cloned.1.call-start = ((), (), s32[]{:S(2)}) async-start(), calls=%async_computation.14 | async-start | bytes 1966080 | tf_op jit(solution)/shard_map/all_gather | solution.py:141
  205.7 85.8 %all-to-all-start.2 = ((bf16[4,1,256,768]{3,2,1,0:T(8,128)(2,1)}), bf16[4,1,256,768]{3,2,1,0:T(8,128)(2,1)}, u32[]{:S(2)}, u32[]{:S(2)}) async-start(bf16[4,1,256,768]{3,2,1,0:T(8,128)(2,1)} %bitcast.520), calls=%async_computation.2 | async-start | bytes 3145728 | tf_op jit(solution)/shard_map/all_to_all | solution.py:234
  291.5 44.7 %all-to-all-start = ((bf16[4,1,256,768]{3,2,1,0:T(8,128)(2,1)}), bf16[4,1,256,768]{3,2,1,0:T(8,128)(2,1)}, u32[]{:S(2)}, u32[]{:S(2)}) async-start(bf16[4,1,256,768]{3,2,1,0:T(8,128)(2,1)} %bitcast.519), calls=%async_computation | async-start | bytes 3145728 | tf_op jit(solution)/shard_map/all_to_all | solution.py:200
  336.2 9.2 copy-start.69
  345.4 12.7 copy-start.62
  364.9 41.1 %all-to-all-start.1 = ((bf16[4,1,256,768]{3,2,1,0:T(8,128)(2,1)}), bf16[4,1,256,768]{3,2,1,0:T(8,128)(2,1)}, u32[]{:S(2)}, u32[]{:S(2)}) async-start(bf16[4,1,256,768]{3,2,1,0:T(8,128)(2,1)} %fusion.90), calls=%async_computation.1 | async-start | bytes 3145728 | tf_op jit(solution)/shard_map/all_to_all | solution.py:205
  383.4 26.2 %copy-start.4 = (bf16[256,768]{1,0:T(8,128)(2,1)S(1)}, bf16[256,768]{1,0:T(8,128)(2,1)}, u32[]{:S(2)}) copy-start(bf16[256,768]{1,0:T(8,128)(2,1)} %copy-done.3) | copy-start | bytes 1179652
  406.0 40.0 %all-to-all-start.3 = ((bf16[4,1,256,768]{3,2,1,0:T(8,128)(2,1)}), bf16[4,1,256,768]{3,2,1,0:T(8,128)(2,1)S(1)}, u32[]{:S(2)}, u32[]{:S(2)}) async-start(bf16[4,1,256,768]{3,2,1,0:T(8,128)(2,1)} %fusion.93), calls=%async_computation.3 | async-start | bytes 3145728 | tf_op jit(solution)/shard_map/all_to_all | solution.py:256
  409.6 160.6 %reduce-scatter.12.cloned.1.call-start = ((), (), s32[]{:S(2)}) async-start(), calls=%async_computation.15 | async-start | bytes 3932160 | tf_op jit(solution)/shard_map/reduce_scatter | solution.py:338
  420.8 9.9 copy-start.17
  480.4 153.2 %reduce-scatter.28.cloned.1.call-start = ((), (), s32[]{:S(2)}) async-start(), calls=%async_computation.23 | async-start | bytes 1622016
  480.5 8.0 copy-start.67
  497.8 277.9 %all-reduce.4.cloned.1.call-start = ((), (), s32[]{:S(2)}) async-start(), calls=%async_computation.24 | async-start | bytes 18874368 | tf_op jit(solution)/shard_map/psum | solution.py:259
  506.3 376.8 %reduce-scatter.20.cloned.1.call-start = ((), (), s32[]{:S(2)}) async-start(), calls=%async_computation.19 | async-start | bytes 3244032 | tf_op jit(solution)/shard_map/reduce_scatter | solution.py:372
  509.7 493.0 %reduce-scatter.22.cloned.1.call-start = ((), (), s32[]{:S(2)}) async-start(), calls=%async_computation.20 | async-start | bytes 6488064 | tf_op jit(solution)/shard_map/reduce_scatter | solution.py:376
  530.6 592.7 %reduce-scatter.24.cloned.1.call-start = ((), (), s32[]{:S(2)}) async-start(), calls=%async_computation.21 | async-start | bytes 6488064 | tf_op jit(solution)/shard_map/reduce_scatter | solution.py:379
  551.4 692.0 %reduce-scatter.26.cloned.1.call-start = ((), (), s32[]{:S(2)}) async-start(), calls=%async_computation.22 | async-start | bytes 6488064 | tf_op jit(solution)/shard_map/reduce_scatter | solution.py:382
  570.1 780.8 %reduce-scatter.14.cloned.1.call-start = ((), (), s32[]{:S(2)}) async-start(), calls=%async_computation.16 | async-start | bytes 3244032 | tf_op jit(solution)/shard_map/reduce_scatter | solution.py:365
  579.7 878.7 %reduce-scatter.16.cloned.1.call-start = ((), (), s32[]{:S(2)}) async-start(), calls=%async_computation.17 | async-start | bytes 3244032 | tf_op jit(solution)/shard_map/reduce_scatter | solution.py:368
  582.1 983.6 %reduce-scatter.18.cloned.1.call-start = ((), (), s32[]{:S(2)}) async-start(), calls=%async_computation.18 | async-start | bytes 3244032 | tf_op jit(solution)/shard_map/reduce_scatter | solution.py:369
  784.8 780.9 %copy-start.1 = (bf16[1,768,2048]{2,1,0:T(8,128)(2,1)S(1)}, bf16[1,768,2048]{2,1,0:T(8,128)(2,1)}, u32[]{:S(2)}) copy-start(bf16[1,768,2048]{2,1,0:T(8,128)(2,1)} %param.31) | copy-start | bytes 9437188
  (67 other events, 211.6 us)
Sparse Core Ops, SparseCore 0:
  21.6 22.3 all-gather.2
  46.1 19.6 all-gather.4
  480.6 50.0 reduce-scatter.11
  536.6 97.0 reduce-scatter.27
  638.0 137.6 all-reduce.3
  781.5 101.5 reduce-scatter.19
  889.3 113.2 reduce-scatter.21
  1009.8 113.4 reduce-scatter.23
  1129.5 113.8 reduce-scatter.25
  1250.1 100.7 reduce-scatter.13
  1357.9 100.4 reduce-scatter.15
  1465.1 100.4 reduce-scatter.17
where the time goes:
time: 1580 us; the launch traced here: 1570 us
  waiting for transfers between devices  1010 us (64%)
  local copies, waits for them, and re-layouts  278 us (18%)
  matrix products  149 us (9%)
  other arithmetic  57.3 us (4%)
  blocking collectives  39.5 us (2%)
  starting transfers between devices  25.2 us (2%)
    scatter x2, local copies, waits for them, and re-layouts, to_slots(): return empty_slots.at[flat_ids, slot_place].set(routed_rows).reshape(exp_...  143 us
    psum x1, waiting for transfers between devices, per_device(): lax.psum(grad_expert_gate.astype(jnp.bfloat16), ('seq', 'ctx'))  141 us
    reduce_scatter x1, waiting for transfers between devices, per_device(): lax.psum_scatter(spread(grad_shared_up), ('seq', 'ctx', 'exp'), scatter_d...  121 us
    reduce_scatter x1, waiting for transfers between devices, per_device(): lax.psum_scatter(spread(grad_shared_down), ('seq', 'ctx', 'exp'), scatter...  120 us
    reduce_scatter x1, waiting for transfers between devices, per_device(): lax.psum_scatter(spread(grad_shared_gate), ('seq', 'ctx', 'exp'), scatter...  120 us
    reduce_scatter x1, waiting for transfers between devices, per_device(): lax.psum_scatter(spread(grad_query), ('seq', 'ctx', 'exp'), scatter_dimen...  108 us
    reduce_scatter x1, waiting for transfers between devices, per_device(): lax.psum_scatter(spread(grad_key), ('seq', 'ctx', 'exp'), scatter_dimensi...  107 us
    reduce_scatter x1, waiting for transfers between devices, per_device(): lax.psum_scatter(spread(grad_value), ('seq', 'ctx', 'exp'), scatter_dimen...  107 us
  transfers between devices with their start and end apart: 16, of which 14 were waited for; matrix products, arithmetic and copies ran while one was open for 16% of the time, Pallas kernels for 0%

commit v1 on v0

--- a/solution.py
+++ b/solution.py
@@ -57,7 +57,7 @@
     return blocks.reshape(col_groups * row_count, col_count // col_groups)
 
 
-def per_device(
+def per_device_slots(
     tokens,
     expert_ids,
     norm_one,
@@ -172,7 +172,10 @@
     slot_hits = (flat_ids[:, None] == jnp.arange(experts_all, dtype=jnp.int32)[None, :]).astype(
         jnp.int32
     )
-    slot_place = jnp.sum((jnp.cumsum(slot_hits, axis=0) - slot_hits) * slot_hits, axis=1)
+    order = jnp.arange(flat_ids.shape[0], dtype=jnp.int32)
+    earlier = (order[None, :] < order[:, None]).astype(jnp.bfloat16)
+    counts_before = product(earlier, slot_hits.astype(jnp.bfloat16)).astype(jnp.int32)
+    slot_place = jnp.sum(counts_before * slot_hits, axis=1)
 
     def to_slots(routed_rows):
         empty_slots = jnp.zeros((experts_all, capacity, model_width), jnp.bfloat16)
@@ -403,7 +406,208 @@
     )
 
 
+def per_device_dense(
+    tokens,
+    expert_ids,
+    norm_one,
+    w_query,
+    w_key,
+    w_value,
+    w_out,
+    norm_two,
+    w_router,
+    expert_gate,
+    expert_up,
+    expert_down,
+    shared_gate,
+    shared_up,
+    shared_down,
+    cotangent,
+):
+    rows = tokens.shape[1]
+    width = tokens.shape[2]
+    heads = width // HEAD_DIM
+    scale = HEAD_DIM ** (-0.5)
+    ctx_count = lax.axis_size("ctx")
+    ctx_place = lax.axis_index("ctx")
+    exp_count = lax.axis_size("exp")
+    exp_place = lax.axis_index("exp")
+    row_groups = lax.axis_size("seq") * ctx_count
+    places = ctx_place * rows + jnp.arange(rows, dtype=jnp.int32)
+    upstream = cotangent[0]
+    ids = expert_ids[0]
+
+    def spread(matrix):
+        return tiled(matrix.astype(jnp.bfloat16), row_groups, exp_count)
+
+    upstream_all = lax.all_gather(upstream, "exp", axis=0, tiled=True)
+    ids_all = lax.all_gather(ids, "exp", axis=0, tiled=True)
+
+    inputs = tokens[0].astype(jnp.float32)
+    normed_full, norm_one_pull = jax.vjp(normalize, inputs, norm_one)
+    normed = normed_full.astype(jnp.bfloat16)
+
+    def heads_of(matrix):
+        return matrix.reshape(matrix.shape[0], heads, HEAD_DIM)
+
+    query = rotate(heads_of(product(normed, w_query)), places).astype(jnp.bfloat16)
+    keys = rotate(heads_of(product(normed, w_key)), places).astype(jnp.bfloat16)
+    values = product(normed, w_value).astype(jnp.bfloat16)
+    both = jnp.concatenate([keys.reshape(rows, width), values], axis=1)
+    both_all = lax.all_gather(both, "ctx", axis=0, tiled=True)
+    keys_all, values_all = heads_of(both_all[:, :width]), heads_of(both_all[:, width:])
+    span = keys_all.shape[0]
+    allowed = (jnp.arange(span, dtype=jnp.int32) // BLOCK)[None, None, :] <= (
+        places // BLOCK
+    )[None, :, None]
+    scores = jnp.einsum("qhd,khd->hqk", query, keys_all, preferred_element_type=jnp.float32)
+    scores = jnp.where(allowed, scores * scale, -1e30)
+    highest = jnp.max(scores, axis=-1, keepdims=True)
+    unscaled = jnp.exp(scores - highest)
+    totals = jnp.sum(unscaled, axis=-1, keepdims=True)
+    weights = unscaled / totals
+    weights_low = weights.astype(jnp.bfloat16)
+    attended = (
+        jnp.einsum("hqk,khd->qhd", weights_low, values_all, preferred_element_type=jnp.float32)
+        .reshape(rows, width)
+        .astype(jnp.bfloat16)
+    )
+    mixed = inputs + product(attended, w_out)
+    second_full, norm_two_pull = jax.vjp(normalize, mixed, norm_two)
+    second = second_full.astype(jnp.bfloat16)
+    experts_all = w_router.shape[1]
+
+    def gates_of(rows_second, rows_ids):
+        logits = product(rows_second, w_router)
+        named = jnp.any(
+            rows_ids[:, :, None] == jnp.arange(experts_all, dtype=jnp.int32)[None, None, :], axis=1
+        )
+        masked = jnp.where(named, logits, -1e30)
+        raised = jnp.where(named, jnp.exp(masked - jnp.max(masked, axis=-1, keepdims=True)), 0.0)
+        return raised / jnp.sum(raised, axis=-1, keepdims=True), named
+
+    shares, named = gates_of(second, ids)
+    second_all = lax.all_gather(second, "exp", axis=0, tiled=True)
+    shares_all, unused = gates_of(second_all, ids_all)
+    mine = (jnp.arange(experts_all, dtype=jnp.int32) == exp_place)[None, :]
+    share = jnp.sum(jnp.where(mine, shares_all, 0.0), axis=1, keepdims=True)
+    gate_w, up_w, down_w = expert_gate[0], expert_up[0], expert_down[0]
+    d_result = (share * upstream_all.astype(jnp.float32)).astype(jnp.bfloat16)
+    gate_pre = product(second_all, gate_w)
+    up_pre = product(second_all, up_w)
+    silu, slope = silu_parts(gate_pre)
+    hidden = (silu * up_pre).astype(jnp.bfloat16)
+    result = product(hidden, down_w).astype(jnp.bfloat16)
+    d_hidden = against(d_result, down_w)
+    d_gate_pre = (d_hidden * up_pre * slope).astype(jnp.bfloat16)
+    d_up_pre = (d_hidden * silu).astype(jnp.bfloat16)
+    d_routed = (against(d_gate_pre, gate_w) + against(d_up_pre, up_w)).astype(jnp.bfloat16)
+    expert_grads = (
+        outer_sum(second_all, d_gate_pre),
+        outer_sum(second_all, d_up_pre),
+        outer_sum(hidden, d_result),
+    )
+    expert_grads = tuple(
+        lax.psum(g.astype(jnp.bfloat16), ("seq", "ctx")).astype(jnp.float32)[None]
+        for g in expert_grads
+    )
+    back = jnp.stack(
+        [result.reshape(exp_count, rows, width), d_routed.reshape(exp_count, rows, width)], axis=1
+    )
+    back = lax.all_to_all(back, "exp", split_axis=0, concat_axis=0, tiled=True)
+    expert_out = back[:, 0].astype(jnp.float32)
+    shared_gate_pre = product(second, shared_gate)
+    shared_up_pre = product(second, shared_up)
+    shared_silu, shared_slope = silu_parts(shared_gate_pre)
+    shared_hidden = (shared_silu * shared_up_pre).astype(jnp.bfloat16)
+    d_shared_hidden = against(upstream, shared_down)
+    d_shared_gate = (d_shared_hidden * shared_up_pre * shared_slope).astype(jnp.bfloat16)
+    d_shared_up = (d_shared_hidden * shared_silu).astype(jnp.bfloat16)
+    grad_shared_gate = outer_sum(second, d_shared_gate)
+    grad_shared_up = outer_sum(second, d_shared_up)
+    grad_shared_down = outer_sum(shared_hidden, upstream)
+    mixture = jnp.sum(shares.T[:, :, None] * expert_out, axis=0)
+    output = (mixed + mixture + product(shared_hidden, shared_down)).astype(jnp.bfloat16)
+    upstream_full = upstream.astype(jnp.float32)
+    d_gates = jnp.sum(upstream_full[None] * expert_out, axis=-1).T
+    d_gates = jnp.where(named, d_gates, 0.0)
+    d_logits = (shares * (d_gates - jnp.sum(shares * d_gates, axis=-1, keepdims=True))).astype(
+        jnp.bfloat16
+    )
+    grad_router = outer_sum(second, d_logits)
+    d_second = (
+        against(d_shared_gate, shared_gate)
+        + against(d_shared_up, shared_up)
+        + against(d_logits, w_router)
+        + jnp.sum(back[:, 1].astype(jnp.float32), axis=0)
+    )
+    d_mixed_part, grad_norm_two = norm_two_pull(d_second)
+    d_mixed = upstream_full + d_mixed_part
+    d_attention = d_mixed.astype(jnp.bfloat16)
+    grad_out = outer_sum(attended, d_attention)
+    d_attended = heads_of(against(d_attention, w_out).astype(jnp.bfloat16))
+    d_weights = jnp.einsum(
+        "qhd,khd->hqk", d_attended, values_all, preferred_element_type=jnp.float32
+    )
+    delta = jnp.sum(weights * d_weights, axis=-1, keepdims=True)
+    d_scores = (weights * (d_weights - delta)).astype(jnp.bfloat16)
+    d_query = (
+        jnp.einsum("hqk,khd->qhd", d_scores, keys_all, preferred_element_type=jnp.float32) * scale
+    )
+    d_key = (
+        jnp.einsum("hqk,qhd->khd", d_scores, query, preferred_element_type=jnp.float32) * scale
+    )
+    d_value = jnp.einsum(
+        "hqk,qhd->khd", weights_low, d_attended, preferred_element_type=jnp.float32
+    )
+    key_terms = jnp.concatenate([d_key.reshape(span, width), d_value.reshape(span, width)], axis=1)
+    key_grads = lax.psum_scatter(
+        key_terms.astype(jnp.bfloat16), "ctx", scatter_dimension=0, tiled=True
+    )
+    d_value = key_grads[:, width:]
+    d_key_lin = rotate(heads_of(key_grads[:, :width].astype(jnp.float32)), -places)
+    d_key_lin = d_key_lin.astype(jnp.bfloat16).reshape(rows, width)
+    d_query_lin = rotate(d_query, -places).astype(jnp.bfloat16).reshape(rows, width)
+    grad_query = outer_sum(normed, d_query_lin)
+    grad_key = outer_sum(normed, d_key_lin)
+    grad_value = outer_sum(normed, d_value)
+    d_normed = against(d_query_lin, w_query) + against(d_key_lin, w_key) + against(d_value, w_value)
+    d_inputs, grad_norm_one = norm_one_pull(d_normed)
+    grad_tokens = (d_mixed + d_inputs)[None]
+    scattered = [
+        lax.psum_scatter(
+            spread(g), ("seq", "ctx", "exp"), scatter_dimension=0, tiled=True
+        ).astype(jnp.float32)
+        for g in (
+            grad_query,
+            grad_key,
+            grad_value,
+            grad_out,
+            grad_router,
+            grad_shared_gate,
+            grad_shared_up,
+            grad_shared_down,
+        )
+    ]
+    grad_norm_one, grad_norm_two = lax.psum((grad_norm_one, grad_norm_two), ("seq", "ctx", "exp"))
+    return (
+        output[None],
+        grad_tokens,
+        grad_norm_one,
+        *scattered[:4],
+        grad_norm_two,
+        scattered[4],
+        *expert_grads,
+        *scattered[5:],
+    )
+
+
+def fits(mesh):
+    return dict(mesh.shape) == {"seq": 2, "ctx": 4, "exp": 4}
+
+
 def solution(mesh):
+    per_device = per_device_dense if fits(mesh) else per_device_slots
     in_specs = (
         P(("seq", "exp"), "ctx", None),
         P(("seq", "exp"), "ctx", None),

time: 1580 us -> 1340 us (0.85)
  local copies, waits for them, and re-layouts: 278 us -> 90.3 us
  waiting for transfers between devices: 1010 us -> 952 us
    scatter x2 -> x0, local copies, waits for them, and re-layouts: 143 us -> none  [to_slots(): return empty_slots.at[flat_ids, slot_place].set(routed_rows).reshape(exp_...]
    reduce_scatter x8, waiting for transfers between devices: 738 us -> 603 us  [the longest x7 603 us: per_device_dense(): lax.psum_scatter(spread(g), ('seq', 'ctx', 'exp'), scatter_dimension=0, t...]
    dot_general x20 -> x5, matrix products: 100 us -> 29.4 us  [the longest x1 9.1 us: per_device_dense(): jnp.einsum('qhd,khd->hqk', d_attended, values_all, preferred_element_type...]
    all_gather x2 -> x3, waiting for transfers between devices: 30.9 us -> 81.1 us  [the longest x1 30.4 us: per_device_dense(): both_all = lax.all_gather(both, 'ctx', axis=0, tiled=True)]
    unnamed x13 -> x14, waiting for transfers between devices: 42.9 us -> 89.2 us
    dot_general x8 -> x12, matrix products: 21.2 us -> 47.6 us  [product(): jnp.dot(first_factor, second_factor, preferred_element_type=jnp.float32)]
    dot_general x8 -> x11, matrix products: 10.4 us -> 29.1 us  [against(): lax.dot_general(first_factor, second_factor, (((1,), (1,)), ((), ())), pr...]
    all_to_all x4 -> x1, starting transfers between devices: 23.4 us -> 4.85 us  [per_device_dense(): back = lax.all_to_all(back, 'exp', split_axis=0, concat_axis=0, tiled=True)]
  transfers between devices with their start and end apart: 16 -> 14, of which waited for: 14 -> 13; matrix products, arithmetic and copies ran while one was open for 16% -> 12% of each run, Pallas kernels for 0% -> 0%
where the time goes in v1:
time: 1340 us; the launch traced here: 1330 us
  waiting for transfers between devices  952 us (71%)
  matrix products  150 us (11%)
  local copies, waits for them, and re-layouts  90.3 us (7%)
  other arithmetic  53 us (4%)
  blocking collectives  52.4 us (4%)
  starting transfers between devices  14.9 us (1%)
  between operations  14.8 us (1%)
    reduce_scatter x7, waiting for transfers between devices, per_device_dense(): lax.psum_scatter(spread(g), ('seq', 'ctx', 'exp'), scatter_dimension=0, t...  603 us
    psum x1, waiting for transfers between devices, per_device_dense(): lax.psum(g.astype(jnp.bfloat16), ('seq', 'ctx')).astype(jnp.float32)[None]  129 us
    unnamed x14, waiting for transfers between devices  89.2 us
    all_to_all x1, waiting for transfers between devices, per_device_dense(): back = lax.all_to_all(back, 'exp', split_axis=0, concat_axis=0, tiled=True)  49.5 us
    dot_general x12, matrix products, product(): jnp.dot(first_factor, second_factor, preferred_element_type=jnp.float32)  47.6 us
    psum x1, blocking collectives, per_device_dense(): lax.psum((grad_norm_one, grad_norm_two), ('seq', 'ctx', 'exp'))  40.1 us
    dot_general x11, matrix products, outer_sum(): lax.dot_general(first_factor, second_factor, (((0,), (0,)), ((), ())), pr...  32.9 us
    all_gather x1, waiting for transfers between devices, per_device_dense(): both_all = lax.all_gather(both, 'ctx', axis=0, tiled=True)  30.4 us
  transfers between devices with their start and end apart: 14, of which 13 were waited for; matrix products, arithmetic and copies ran while one was open for 12% of the time, Pallas kernels for 0%

profile of v1, /device:TPU:0, one launch (start us, length us, event | category | flops | bytes accessed | tf_op | source)
XLA Modules:
  0.0 1327.1 jit_solution(8332515042756077611)
XLA Ops:
  29.9 30.4 %all-gather.6.cloned.1.call-done = bf16[1024,1536]{1,0:T(8,128)(2,1)} async-done(((bf16[256,1536]{1,0:T(8,128)(2,1)}), bf16[1024,1536]{1,0:T(8,128)(2,1)}) %all-gather.6.cloned.1.call-update) | async-done | bytes 3145744 | tf_op jit(solution)/shard_map/all_gather | solution.py:457
  69.2 11.2 fusion.107
  80.4 7.2 fusion.41
  90.9 12.3 all-gather
  103.2 24.2 %all-gather.8.cloned.1.call-done = bf16[1024,768]{1,0:T(8,128)(2,1)} async-done(((bf16[256,768]{1,0:T(8,128)(2,1)}), bf16[1024,768]{1,0:T(8,128)(2,1)}) %all-gather.8.cloned.1.call-update) | async-done | bytes 1572880 | tf_op jit(solution)/shard_map/all_gather | solution.py:490
  129.5 9.0 fusion.19
  138.5 26.5 %all-gather.10.cloned.1.call-done = bf16[1,1024,768]{2,1,0:T(8,128)(2,1)} async-done(((bf16[1,256,768]{2,1,0:T(8,128)(2,1)}), bf16[1,1024,768]{2,1,0:T(8,128)(2,1)}) %all-gather.10.cloned.1.call-update) | async-done | bytes 1572880 | tf_op jit(solution)/shard_map/all_gather | solution.py:443
  165.0 9.2 fusion.9
  174.2 11.5 multiply_convert_fusion.3
  185.7 8.5 fusion.34
  208.1 8.7 reduce-scatter.12.cloned.1.call-start
  229.5 49.5 %all-to-all-done = bf16[4,2,256,768]{3,2,1,0:T(8,128)(2,1)} async-done(((bf16[4,2,256,768]{3,2,1,0:T(8,128)(2,1)}), bf16[4,2,256,768]{3,2,1,0:T(8,128)(2,1)}, u32[]{:S(2)}, u32[]{:S(2)}) %all-to-all-start) | async-done | bytes 3145760 | tf_op jit(solution)/shard_map/all_to_all | solution.py:517
  292.3 9.1 multiply_reduce_fusion
  366.3 7.3 fusion.25
  414.6 42.5 %reduce-scatter.24.cloned.1.call-done = bf16[96,512]{1,0:T(8,128)(2,1)} async-done(((bf16[3072,512]{1,0:T(8,128)(2,1)}), bf16[96,512]{1,0:T(8,128)(2,1)}) %reduce-scatter.24.cloned.1.call-update) | async-done | bytes 98320 | tf_op jit(solution)/shard_map/reduce_scatter | solution.py:578
  458.7 105.1 %reduce-scatter.22.cloned.1.call-done = bf16[96,512]{1,0:T(8,128)(2,1)} async-done(((bf16[3072,512]{1,0:T(8,128)(2,1)}), bf16[96,512]{1,0:T(8,128)(2,1)}) %reduce-scatter.22.cloned.1.call-update) | async-done | bytes 98320 | tf_op jit(solution)/shard_map/reduce_scatter | solution.py:578
  565.4 105.2 %reduce-scatter.26.cloned.1.call-done = bf16[256,192]{0,1:T(8,128)(2,1)} async-done(((bf16[8192,192]{0,1:T(8,128)(2,1)}), bf16[256,192]{0,1:T(8,128)(2,1)}) %reduce-scatter.26.cloned.1.call-update) | async-done | bytes 98320 | tf_op jit(solution)/shard_map/reduce_scatter | solution.py:578
  684.2 129.0 %all-reduce.4.cloned.1.call-done = (bf16[1,768,2048]{2,1,0:T(8,128)(2,1)}, bf16[1,768,2048]{2,1,0:T(8,128)(2,1)}, bf16[1,2048,768]{2,1,0:T(8,128)(2,1)}) async-done(((bf16[1,768,2048]{2,1,0:T(8,128)(2,1)}, bf16[1,768,2048]{2,1,0:T(8,128)(2,1)}, bf16[1,2048,768]{2,1,0:T(8,128)(2,1)}), (bf16[1,768,2048]{2,1,0:T(8,128)(2,1)}, bf16[1,768,2048]{2,1,0:T(8,128)(2,1)}, ...) | async-done | bytes 9437200 | tf_op jit(solution)/shard_map/psum | solution.py:511
  825.6 88.4 %reduce-scatter.28.cloned.1.call-done = bf16[96,1]{1,0:T(8,128)(2,1)} async-done(((bf16[3072,1]{1,0:T(8,128)(2,1)}), bf16[96,1]{1,0:T(8,128)(2,1)}) %reduce-scatter.28.cloned.1.call-update) | async-done | bytes 208
  915.2 99.8 %reduce-scatter.20.cloned.1.call-done = bf16[96,192]{1,0:T(8,128)(2,1)} async-done(((bf16[3072,192]{1,0:T(8,128)(2,1)}), bf16[96,192]{1,0:T(8,128)(2,1)}) %reduce-scatter.20.cloned.1.call-update) | async-done | bytes 36880 | tf_op jit(solution)/shard_map/reduce_scatter | solution.py:578
  1022.6 40.1 %all-reduce = (f32[768]{0:T(1024)}, f32[768]{0:T(1024)}) all-reduce(f32[768]{0:T(1024)S(1)} %get-tuple-element.19, f32[768]{0:T(1024)S(1)} %get-tuple-element.17), channel_id=1, replica_groups=mesh['seq'=2,'ctx'=4,'exp'=4] {'seq','ctx','exp'}, use_global_device_ids=true, to_apply=%region_20.21 | all-reduce | flops 1536 | bytes 12288 | tf_op jit(solution)/shard_map/psum | solution.py:592
  1065.9 50.5 %reduce-scatter.18.cloned.1.call-done = bf16[96,192]{1,0:T(8,128)(2,1)} async-done(((bf16[3072,192]{1,0:T(8,128)(2,1)}), bf16[96,192]{1,0:T(8,128)(2,1)}) %reduce-scatter.18.cloned.1.call-update) | async-done | bytes 36880 | tf_op jit(solution)/shard_map/reduce_scatter | solution.py:578
  1117.9 99.7 %reduce-scatter.16.cloned.1.call-done = bf16[96,192]{1,0:T(8,128)(2,1)} async-done(((bf16[3072,192]{1,0:T(8,128)(2,1)}), bf16[96,192]{1,0:T(8,128)(2,1)}) %reduce-scatter.16.cloned.1.call-update) | async-done | bytes 36880 | tf_op jit(solution)/shard_map/reduce_scatter | solution.py:578
  1219.0 99.9 %reduce-scatter.14.cloned.1.call-done = bf16[96,192]{1,0:T(8,128)(2,1)} async-done(((bf16[3072,192]{1,0:T(8,128)(2,1)}), bf16[96,192]{1,0:T(8,128)(2,1)}) %reduce-scatter.14.cloned.1.call-update) | async-done | bytes 36880 | tf_op jit(solution)/shard_map/reduce_scatter | solution.py:578
  (253 shorter events, 227.5 us)
Async XLA Ops:
  7.2 167.0 %copy-start = (bf16[1,768,2048]{2,1,0:T(8,128)(2,1)S(1)}, bf16[1,768,2048]{2,1,0:T(8,128)(2,1)}, u32[]{:S(2)}) copy-start(bf16[1,768,2048]{2,1,0:T(8,128)(2,1)} %param.26) | copy-start | bytes 9437188
  7.2 53.1 %all-gather.6.cloned.1.call-start = ((), (), s32[]{:S(2)}) async-start(), calls=%async_computation.10 | async-start | bytes 3932160 | tf_op jit(solution)/shard_map/all_gather | solution.py:457
  28.9 98.5 %all-gather.8.cloned.1.call-start = ((), (), s32[]{:S(2)}) async-start(), calls=%async_computation.11 | async-start | bytes 1966080 | tf_op jit(solution)/shard_map/all_gather | solution.py:490
  87.6 39.8 %copy-start.39 = (bf16[768,4]{0,1:T(4,128)(2,1)S(1)}, bf16[768,4]{0,1:T(4,128)(2,1)}, u32[]{:S(2)}) copy-start(bf16[768,4]{0,1:T(4,128)(2,1)} %param.24) | copy-start | bytes 18436
  90.1 74.8 %all-gather.10.cloned.1.call-start = ((), (), s32[]{:S(2)}) async-start(), calls=%async_computation.20 | async-start | bytes 1966080 | tf_op jit(solution)/shard_map/all_gather | solution.py:443
  185.7 12.1 copy-start.54
  203.2 13.6 %copy-start.11 = (bf16[1,256,768]{2,1,0:T(8,128)(2,1)S(1)}, bf16[1,256,768]{2,1,0:T(8,128)(2,1)}, u32[]{:S(2)}) copy-start(bf16[1,256,768]{2,1,0:T(8,128)(2,1)} %param.31) | copy-start | bytes 1179652
  203.2 13.7 %copy-start.3 = (bf16[256,768]{1,0:T(8,128)(2,1)S(1)}, bf16[256,768]{1,0:T(8,128)(2,1)}, u32[]{:S(2)}) copy-start(bf16[256,768]{1,0:T(8,128)(2,1)} %multiply_convert_fusion.8) | copy-start | bytes 1179652
  203.2 75.8 %all-to-all-start = ((bf16[4,2,256,768]{3,2,1,0:T(8,128)(2,1)}), bf16[4,2,256,768]{3,2,1,0:T(8,128)(2,1)}, u32[]{:S(2)}, u32[]{:S(2)}) async-start(bf16[4,2,256,768]{3,2,1,0:T(8,128)(2,1)} %pad_maximum_fusion), calls=%async_computation | async-start | bytes 6291456 | tf_op jit(solution)/shard_map/all_to_all | solution.py:517
  208.1 185.2 %reduce-scatter.12.cloned.1.call-start = ((), (), s32[]{:S(2)}) async-start(), calls=%async_computation.12 | async-start | bytes 3932160 | tf_op jit(solution)/shard_map/reduce_scatter | solution.py:564
  229.5 54.6 %copy-start.7 = (f32[256,768]{1,0:T(8,128)S(1)}, f32[256,768]{1,0:T(8,128)}, u32[]{:S(2)}) copy-start(f32[256,768]{1,0:T(8,128)} %copy-done.6) | copy-start | bytes 2359300
  286.0 15.4 %slice-start = ((s8[12582912]{0:T(1024)(128)(4,1)}), s8[4194304]{0:T(1024)(128)(4,1)S(1)}, s32[]{:S(2)}) async-start(s8[12582912]{0:T(1024)(128)(4,1)} %bitcast.231), calls=%async_computation.23 | async-start | bytes 8388608
  286.0 15.4 %slice-start.1 = ((s8[12582912]{0:T(1024)(128)(4,1)}), s8[4194304]{0:T(1024)(128)(4,1)S(1)}, s32[]{:S(2)}) async-start(s8[12582912]{0:T(1024)(128)(4,1)} %bitcast.231), calls=%async_computation.24 | async-start | bytes 8388608
  312.2 144.9 %reduce-scatter.24.cloned.1.call-start = ((), (), s32[]{:S(2)}) async-start(), calls=%async_computation.18 | async-start | bytes 3244032 | tf_op jit(solution)/shard_map/reduce_scatter | solution.py:578
  326.8 236.9 %reduce-scatter.22.cloned.1.call-start = ((), (), s32[]{:S(2)}) async-start(), calls=%async_computation.17 | async-start | bytes 3244032 | tf_op jit(solution)/shard_map/reduce_scatter | solution.py:578
  341.4 329.2 %reduce-scatter.26.cloned.1.call-start = ((), (), s32[]{:S(2)}) async-start(), calls=%async_computation.19 | async-start | bytes 3244032 | tf_op jit(solution)/shard_map/reduce_scatter | solution.py:578
  364.9 448.3 %all-reduce.4.cloned.1.call-start = ((), (), s32[]{:S(2)}) async-start(), calls=%async_computation.22 | async-start | bytes 18874368 | tf_op jit(solution)/shard_map/psum | solution.py:511
  383.6 530.3 %reduce-scatter.28.cloned.1.call-start = ((), (), s32[]{:S(2)}) async-start(), calls=%async_computation.21 | async-start | bytes 811008
  386.5 628.6 %reduce-scatter.20.cloned.1.call-start = ((), (), s32[]{:S(2)}) async-start(), calls=%async_computation.16 | async-start | bytes 1622016 | tf_op jit(solution)/shard_map/reduce_scatter | solution.py:578
  393.2 723.3 %reduce-scatter.18.cloned.1.call-start = ((), (), s32[]{:S(2)}) async-start(), calls=%async_computation.15 | async-start | bytes 1622016 | tf_op jit(solution)/shard_map/reduce_scatter | solution.py:578
  400.9 816.7 %reduce-scatter.16.cloned.1.call-start = ((), (), s32[]{:S(2)}) async-start(), calls=%async_computation.14 | async-start | bytes 1622016 | tf_op jit(solution)/shard_map/reduce_scatter | solution.py:578
  414.6 904.3 %reduce-scatter.14.cloned.1.call-start = ((), (), s32[]{:S(2)}) async-start(), calls=%async_computation.13 | async-start | bytes 1622016 | tf_op jit(solution)/shard_map/reduce_scatter | solution.py:578
  822.4 194.2 %copy-start.14 = (bf16[768,768]{1,0:T(8,128)(2,1)S(1)}, bf16[768,768]{1,0:T(8,128)(2,1)}, u32[]{:S(2)}) copy-start(bf16[768,768]{1,0:T(8,128)(2,1)} %param.19) | copy-start | bytes 3538948
  1017.1 303.3 %copy-start.1 = (bf16[1,768,2048]{2,1,0:T(8,128)(2,1)S(1)}, bf16[1,768,2048]{2,1,0:T(8,128)(2,1)}, u32[]{:S(2)}) copy-start(bf16[1,768,2048]{2,1,0:T(8,128)(2,1)} %param.26) | copy-start | bytes 9437188
  (50 other events, 222.4 us)
Sparse Core Ops, SparseCore 0:
  29.0 31.2 all-gather.5
  90.3 37.1 all-gather.7
  129.0 35.9 all-gather.9
  312.3 36.9 reduce-scatter.11
  355.5 101.5 reduce-scatter.23
  463.3 100.4 reduce-scatter.21
  570.1 100.3 reduce-scatter.25
  675.6 137.5 all-reduce.3
  818.3 95.5 reduce-scatter.27
  919.0 96.0 reduce-scatter.19
  1020.3 96.0 reduce-scatter.17
  1121.5 96.0 reduce-scatter.15
  1222.8 96.0 reduce-scatter.13

commit v2 on v1

--- a/solution.py
+++ b/solution.py
@@ -1,14 +1,18 @@
+import functools
 import math
 
 import jax
 import jax.numpy as jnp
 from jax import lax
+from jax.experimental import pallas as pl
+from jax.experimental.pallas import tpu as pltpu
 from jax.sharding import PartitionSpec as P
 
 HEAD_DIM = 64
 TOP = 2
 BLOCK = 256
 KEY_ROWS = 512
+MESH = pl.DeviceIdType.MESH
 
 
 def product(first_factor, second_factor):
@@ -406,6 +410,226 @@
     )
 
 
+def add_blocks(target, first, second, count, height, step):
+    chunks = height // step
+
+    def body(number, carry):
+        j = number // chunks
+        at = pl.ds(pl.multiple_of((number % chunks) * step, step), step)
+        total = first[j, at, :].astype(jnp.float32) + second[j, at, :].astype(jnp.float32)
+        target[j, at, :] = total.astype(target.dtype)
+        return carry
+
+    lax.fori_loop(0, count * chunks, body, 0)
+
+
+def reduce_kernel(shapes, expert_count, *refs):
+    number = len(shapes)
+    plain = number - expert_count
+    refs = list(refs)
+
+    def take(n):
+        out = refs[:n]
+        del refs[:n]
+        return out
+
+    grads = take(number)
+    (misc_in,) = take(1)
+    whole = take(expert_count)
+    owned = take(plain)
+    (misc_out,) = take(1)
+    own = take(number)
+    got1 = take(number)
+    got2 = take(number)
+    got3 = take(number)
+    zsend = take(plain)
+    zgot = take(plain)
+    misc_got, own_sem = take(2)
+    sem1, rem1, sem2, rem2, sem3, rem3 = take(6)
+    gsem, grem, lsem, zsem, zrem, msem, mrem = take(7)
+
+    s = lax.axis_index("seq")
+    c = lax.axis_index("ctx")
+    e = lax.axis_index("exp")
+    x, k = c // 2, c % 2
+    to_core = (s, x * 2 + (1 - k), e)
+    to_x = (s, (1 - x) * 2 + k, e)
+    to_y = (1 - s, c, e)
+    to_z = [(s, c, lax.rem(e + d, 4)) for d in (1, 2, 3)]
+
+    barrier = pltpu.get_barrier_semaphore()
+    for device in (to_core, to_x, to_y, *to_z):
+        pl.semaphore_signal(barrier, inc=1, device_id=device, device_id_type=MESH)
+    pl.semaphore_wait(barrier, 6)
+
+    def send(src, dst, ssem, rsem, device):
+        copy = pltpu.make_async_remote_copy(
+            src_ref=src, dst_ref=dst, send_sem=ssem, recv_sem=rsem, device_id=device, device_id_type=MESH
+        )
+        copy.start()
+        return copy
+
+    copies = []
+    first = []
+    for i in range(number):
+        local = pltpu.make_async_copy(grads[i].at[:, :, k], own[i], own_sem.at[i])
+        local.start()
+        first.append(
+            (local, send(grads[i].at[:, :, 1 - k], got1[i], sem1.at[i], rem1.at[i], to_core))
+        )
+    mcopy = send(misc_in, misc_got.at[0], msem.at[0], mrem.at[0], to_core)
+    second = []
+    for i in range(number):
+        rows, width = shapes[i]
+        half = rows // 2
+        local, copy = first[i]
+        local.wait()
+        copy.wait()
+        for a in range(2):
+            add_blocks(got1[i].at[a], got1[i].at[a], own[i].at[a], 2, rows, half)
+        second.append(
+            (
+                send(got1[i].at[:, 1 - x, pl.ds(0, half)], got2[i].at[0], sem2.at[i, 0], rem2.at[i, 0], to_x),
+                send(got1[i].at[1 - s, :, pl.ds(half, half)], got2[i].at[1], sem2.at[i, 1], rem2.at[i, 1], to_y),
+            )
+        )
+    mcopy.wait()
+    misc_out[...] = misc_in[...] + misc_got[0]
+    mcopy = send(misc_out, misc_got.at[1], msem.at[1], mrem.at[1], to_x)
+    third = []
+    for i in range(number):
+        rows, width = shapes[i]
+        half = rows // 2
+        second[i][0].wait()
+        add_blocks(got2[i].at[0], got2[i].at[0], got1[i].at[:, x, pl.ds(0, half)], 2, half, half)
+        second[i][1].wait()
+        add_blocks(got2[i].at[1], got2[i].at[1], got1[i].at[s, :, pl.ds(half, half)], 2, half, half)
+        third.append(
+            (
+                send(got2[i].at[0, 1 - s], got3[i].at[0], sem3.at[i, 0], rem3.at[i, 0], to_y),
+                send(got2[i].at[1, 1 - x], got3[i].at[1], sem3.at[i, 1], rem3.at[i, 1], to_x),
+            )
+        )
+    mcopy.wait()
+    misc_got[3] = misc_out[...] + misc_got[1]
+    mcopy = send(misc_got.at[3], misc_got.at[2], msem.at[2], mrem.at[2], to_y)
+    gather = []
+    zcopies = []
+    for i in range(number):
+        rows, width = shapes[i]
+        half = rows // 2
+        third[i][0].wait()
+        third[i][1].wait()
+        mine = (got2[i].at[0, s], got2[i].at[1, x])
+        if i < expert_count:
+            legs = []
+            for h in range(2):
+                got3[i][h] = (got3[i][h].astype(jnp.float32) + mine[h][...].astype(jnp.float32)).astype(jnp.bfloat16)
+                here = whole[i].at[s, x, k, pl.ds(h * half, half)]
+                local = pltpu.make_async_copy(got3[i].at[h], here, lsem.at[i, h])
+                local.start()
+                legs.append(
+                    (
+                        local,
+                        send(got3[i].at[h], here, gsem.at[i, h, 0], grem.at[i, h, 0], (to_y, to_x)[h]),
+                        send(got3[i].at[h], here, gsem.at[i, h, 1], grem.at[i, h, 1], (to_x, to_y)[h]),
+                    )
+                )
+            gather.append(legs)
+        else:
+            j = i - expert_count
+            columns = width // 4
+            for h in range(2):
+                total = (got3[i][h].astype(jnp.float32) + mine[h][...].astype(jnp.float32)).astype(jnp.bfloat16)
+                for q in range(4):
+                    zsend[j][q, pl.ds(h * half, half), :] = total[:, q * columns : (q + 1) * columns]
+            zcopies.append(
+                [
+                    send(zsend[j].at[lax.rem(e + d, 4)], zgot[j].at[d - 1], zsem.at[j, d - 1], zrem.at[j, d - 1], to_z[d - 1])
+                    for d in (1, 2, 3)
+                ]
+            )
+    mcopy.wait()
+    misc_got[4] = misc_got[3] + misc_got[2]
+    mz = [
+        send(misc_got.at[4], misc_got.at[5 + d], msem.at[3 + d], mrem.at[3 + d], to_z[d]) for d in range(3)
+    ]
+    onward = []
+    for i in range(expert_count):
+        half = shapes[i][0] // 2
+        legs = []
+        for h in range(2):
+            gather[i][h][1].wait()
+            part = pl.ds(h * half, half)
+            there = whole[i].at[(1 - s, s)[h], (x, 1 - x)[h], k, part]
+            legs.append(send(there, there, gsem.at[i, h, 2], grem.at[i, h, 2], (to_x, to_y)[h]))
+        onward.append(legs)
+    last = []
+    for i in range(expert_count):
+        for h in range(2):
+            gather[i][h][0].wait()
+            gather[i][h][2].wait()
+            onward[i][h].wait()
+        last.append(send(whole[i].at[:, :, k], whole[i].at[:, :, k], gsem.at[i, 0, 3], grem.at[i, 0, 3], to_core))
+    for j in range(plain):
+        for copy in zcopies[j]:
+            copy.wait()
+        owned[j][...] = (
+            zsend[j][e].astype(jnp.float32)
+            + zgot[j][0].astype(jnp.float32)
+            + zgot[j][1].astype(jnp.float32)
+            + zgot[j][2].astype(jnp.float32)
+        )
+    for copy in mz:
+        copy.wait()
+    misc_out[...] = misc_got[4] + misc_got[5] + misc_got[6] + misc_got[7]
+    for copy in last:
+        copy.wait()
+
+
+def reduce_grads(expert_grads, plain_grads, misc):
+    def blocks(matrix):
+        return matrix.reshape(2, 2, 2, matrix.shape[0] // 8, matrix.shape[1])
+
+    arrays = [blocks(m) for m in (*expert_grads, *plain_grads)]
+    shapes = [(a.shape[3], a.shape[4]) for a in arrays]
+    count, plain = len(expert_grads), len(plain_grads)
+    low, full = jnp.bfloat16, jnp.float32
+    vmem, dma = pltpu.VMEM, pltpu.SemaphoreType.DMA
+    n = len(arrays)
+    in_specs = [pl.BlockSpec(memory_space=pl.ANY)] * n + [pl.BlockSpec(memory_space=pltpu.VMEM)]
+    out_shape = (
+        [jax.ShapeDtypeStruct(a.shape, low) for a in arrays[:count]]
+        + [jax.ShapeDtypeStruct((r, w // 4), full) for r, w in shapes[count:]]
+        + [jax.ShapeDtypeStruct(misc.shape, full)]
+    )
+    out_specs = [pl.BlockSpec(memory_space=pl.ANY)] * count + [pl.BlockSpec(memory_space=pltpu.VMEM)] * (plain + 1)
+    scratch = (
+        [vmem((2, 2, r, w), low) for r, w in shapes]
+        + [vmem((2, 2, r, w), low) for r, w in shapes]
+        + [vmem((2, 2, r // 2, w), low) for r, w in shapes]
+        + [vmem((2, r // 2, w), low) for r, w in shapes]
+        + [vmem((4, r, w // 4), low) for r, w in shapes[count:]]
+        + [vmem((3, r, w // 4), low) for r, w in shapes[count:]]
+        + [vmem((8, *misc.shape), full), dma((n,))]
+        + [dma((n,)), dma((n,)), dma((n, 2)), dma((n, 2)), dma((n, 2)), dma((n, 2))]
+        + [dma((count, 2, 4)), dma((count, 2, 4)), dma((count, 2)), dma((plain, 3)), dma((plain, 3)), dma((6,)), dma((6,))]
+    )
+    results = pl.pallas_call(
+        functools.partial(reduce_kernel, shapes, count),
+        out_shape=out_shape,
+        in_specs=in_specs,
+        out_specs=out_specs,
+        scratch_shapes=scratch,
+        compiler_params=pltpu.CompilerParams(
+            collective_id=1, has_side_effects=True, vmem_limit_bytes=58 * 2**20
+        ),
+        name="reduce_grads",
+    )(*arrays, misc)
+    whole = [r.reshape(g.shape) for r, g in zip(results[:count], expert_grads)]
+    return whole, results[count : count + plain], results[-1]
+
+
 def per_device_dense(
     tokens,
     expert_ids,
@@ -437,9 +661,6 @@
     upstream = cotangent[0]
     ids = expert_ids[0]
 
-    def spread(matrix):
-        return tiled(matrix.astype(jnp.bfloat16), row_groups, exp_count)
-
     upstream_all = lax.all_gather(upstream, "exp", axis=0, tiled=True)
     ids_all = lax.all_gather(ids, "exp", axis=0, tiled=True)
 
@@ -507,10 +728,6 @@
         outer_sum(second_all, d_up_pre),
         outer_sum(hidden, d_result),
     )
-    expert_grads = tuple(
-        lax.psum(g.astype(jnp.bfloat16), ("seq", "ctx")).astype(jnp.float32)[None]
-        for g in expert_grads
-    )
     back = jnp.stack(
         [result.reshape(exp_count, rows, width), d_routed.reshape(exp_count, rows, width)], axis=1
     )
@@ -574,31 +791,36 @@
     d_normed = against(d_query_lin, w_query) + against(d_key_lin, w_key) + against(d_value, w_value)
     d_inputs, grad_norm_one = norm_one_pull(d_normed)
     grad_tokens = (d_mixed + d_inputs)[None]
-    scattered = [
-        lax.psum_scatter(
-            spread(g), ("seq", "ctx", "exp"), scatter_dimension=0, tiled=True
-        ).astype(jnp.float32)
+    misc = jnp.concatenate(
+        [grad_norm_one[None], grad_norm_two[None], grad_router.T, jnp.zeros((2, width), jnp.float32)],
+        axis=0,
+    )
+    low = [g.astype(jnp.bfloat16) for g in expert_grads]
+    plain = [
+        g.astype(jnp.bfloat16)
         for g in (
             grad_query,
             grad_key,
             grad_value,
             grad_out,
-            grad_router,
             grad_shared_gate,
             grad_shared_up,
             grad_shared_down,
         )
     ]
-    grad_norm_one, grad_norm_two = lax.psum((grad_norm_one, grad_norm_two), ("seq", "ctx", "exp"))
+    whole, owned, misc = reduce_grads(low, plain, misc)
+    row_place = lax.axis_index("seq") * ctx_count + ctx_place
+    own_rows = width // row_groups
+    router = lax.dynamic_slice(misc, (2 + exp_place, row_place * own_rows), (1, own_rows))
     return (
         output[None],
         grad_tokens,
-        grad_norm_one,
-        *scattered[:4],
-        grad_norm_two,
-        scattered[4],
-        *expert_grads,
-        *scattered[5:],
+        misc[0],
+        *owned[:4],
+        misc[1],
+        router.T,
+        *[g.astype(jnp.float32)[None] for g in whole],
+        *owned[4:],
     )
 
 

time: 1340 us -> 546 us (0.41)
  waiting for transfers between devices: 952 us -> 144 us
  Pallas kernels: 0 us -> 150 us
  local copies, waits for them, and re-layouts: 90.3 us -> 35 us
  blocking collectives: 52.4 us -> 12.4 us
  matrix products: 150 us -> 134 us
    reduce_scatter x7 -> x0, waiting for transfers between devices: 603 us -> none  [per_device_dense(): lax.psum_scatter(spread(g), ('seq', 'ctx', 'exp'), scatter_dimension=0, t...]
    pallas_call x0 -> x1, Pallas kernels: none -> 150 us  [reduce_grads(): pl.pallas_call(functools.partial(reduce_kernel, shapes, count), out_shape...]
    psum x1 -> x0, waiting for transfers between devices: 129 us -> none  [per_device_dense(): lax.psum(g.astype(jnp.bfloat16), ('seq', 'ctx')).astype(jnp.float32)[None]]
    unnamed x14 -> x4, waiting for transfers between devices: 89.2 us -> 0.73 us
    psum x1 -> x0, blocking collectives: 40.1 us -> none  [per_device_dense(): lax.psum((grad_norm_one, grad_norm_two), ('seq', 'ctx', 'exp'))]
    reshape x9 -> x2, local copies, waits for them, and re-layouts: 35.3 us -> 0.01 us  [normalize(): values * lax.rsqrt(jnp.mean(values * values, axis=-1, keepdims=True) + 1e...]
    transpose x8 -> x1, local copies, waits for them, and re-layouts: 20.4 us -> 1.28 us  [per_device_dense(): return (output[None], grad_tokens, misc[0], *owned[:4], misc[1], router.T...]
  transfers between devices with their start and end apart: 14 -> 5, of which waited for: 13 -> 5; matrix products, arithmetic and copies ran while one was open for 12% -> 10% of each run, Pallas kernels for 0% -> 0%
where the time goes in v2:
time: 546 us; the launch traced here: 538 us
  Pallas kernels  150 us (27%)
  waiting for transfers between devices  144 us (26%)
  matrix products  134 us (25%)
  other arithmetic  42.5 us (8%)
  local copies, waits for them, and re-layouts  35 us (6%)
  between operations  15.3 us (3%)
  blocking collectives  12.4 us (2%)
    pallas_call x1, Pallas kernels, reduce_grads(): pl.pallas_call(functools.partial(reduce_kernel, shapes, count), out_shape...  150 us
    all_to_all x1, waiting for transfers between devices, per_device_dense(): back = lax.all_to_all(back, 'exp', split_axis=0, concat_axis=0, tiled=True)  59.4 us
    dot_general x12, matrix products, product(): jnp.dot(first_factor, second_factor, preferred_element_type=jnp.float32)  38.4 us
    dot_general x11, matrix products, outer_sum(): lax.dot_general(first_factor, second_factor, (((0,), (0,)), ((), ())), pr...  32 us
    all_gather x1, waiting for transfers between devices, per_device_dense(): both_all = lax.all_gather(both, 'ctx', axis=0, tiled=True)  30.4 us
    dot_general x11, matrix products, against(): lax.dot_general(first_factor, second_factor, (((1,), (1,)), ((), ())), pr...  26.8 us
    all_gather x1, waiting for transfers between devices, per_device_dense(): upstream_all = lax.all_gather(upstream, 'exp', axis=0, tiled=True)  25.2 us
    all_gather x1, waiting for transfers between devices, per_device_dense(): second_all = lax.all_gather(second, 'exp', axis=0, tiled=True)  23.6 us
  transfers between devices with their start and end apart: 5, of which 5 were waited for; matrix products, arithmetic and copies ran while one was open for 10% of the time, Pallas kernels for 0%

profile of v2, /device:TPU:0, one launch (start us, length us, event | category | flops | bytes accessed | tf_op | source)
XLA Modules:
  0.0 537.5 jit_solution(13697583706221419670)
XLA Ops:
  29.9 30.4 %all-gather.6.cloned.1.call-done = bf16[1024,1536]{1,0:T(8,128)(2,1)} async-done(((bf16[256,1536]{1,0:T(8,128)(2,1)}), bf16[1024,1536]{1,0:T(8,128)(2,1)}) %all-gather.6.cloned.1.call-update) | async-done | bytes 3145744 | tf_op jit(solution)/shard_map/all_gather | solution.py:678
  60.3 3.7 fusion.103
  69.2 10.6 %fusion.104 = (f32[12,256]{1,0:T(8,128)S(1)}, f32[12,256,1024]{2,1,0:T(8,128)}) fusion(pred[256,1024]{1,0:T(8,128)(4,1)} %broadcast_compare_fusion, bf16[1024,12,64]{0,2,1:T(8,128)(2,1)} %bitcast.225, bf16[256,12,32]{0,2,1:T(8,128)(2,1)} %get-tuple-element.118, bf16[256,12,32]{0,2,1:T(8,128)(2,1)} %get-tuple-element.117), kind=kOutput, calls=%fused_computation.184 | convolution fusion | flops 416023552 | bytes 14823424 | tf_op jit(solution)/shard_map/sub | solution.py:687
  80.5 7.2 %fusion.38 = bf16[12,64,256]{2,1,0:T(8,128)(2,1)S(1)} fusion(bf16[1024,12,64]{0,2,1:T(8,128)(2,1)} %bitcast.243, f32[12,256,1024]{2,1,0:T(8,128)} %get-tuple-element.132, f32[12,256]{1,0:T(8,128)S(1)} %get-tuple-element.131), kind=kOutput, calls=%fused_computation.70 | convolution fusion | flops 409141248 | bytes 14561280 | tf_op jit(solution)/shard_map/hqk,khd->qhd/dot_general | solution.py:692
  91.3 12.4 %all-gather = s32[1,1024,2]{1,2,0:T(2,128)S(1)} all-gather(s32[1,256,2]{1,2,0:T(2,128)S(1)} %copy-done.64), channel_id=2, replica_groups=mesh['seq'=2,'ctx'=4,'exp'=4] {'exp'}, dimensions={1}, use_global_device_ids=true | all-gather | bytes 10240 | tf_op jit(solution)/shard_map/all_gather | solution.py:665
  104.2 23.6 %all-gather.8.cloned.1.call-done = bf16[1024,768]{1,0:T(8,128)(2,1)} async-done(((bf16[256,768]{1,0:T(8,128)(2,1)}), bf16[1024,768]{1,0:T(8,128)(2,1)}) %all-gather.8.cloned.1.call-update) | async-done | bytes 1572880 | tf_op jit(solution)/shard_map/all_gather | solution.py:711
  131.1 9.0 %fusion.19 = f32[1024,2048]{1,0:T(8,128)} fusion(bf16[1024,768]{1,0:T(8,128)(2,1)} %all-gather.8.cloned.1.call-done, bf16[1,768,2048]{2,1,0:T(8,128)(2,1)} %param.25), kind=kOutput, calls=%fused_computation.39 | convolution fusion | flops 3221225472 | bytes 13107200 | tf_op jit(solution)/shard_map/dot_general | solution.py:19
  140.2 25.2 %all-gather.10.cloned.1.call-done = bf16[1,1024,768]{2,1,0:T(8,128)(2,1)} async-done(((bf16[1,256,768]{2,1,0:T(8,128)(2,1)}), bf16[1,1024,768]{2,1,0:T(8,128)(2,1)}) %all-gather.10.cloned.1.call-update) | async-done | bytes 1572880 | tf_op jit(solution)/shard_map/all_gather | solution.py:664
  165.4 9.3 %fusion.9 = f32[1024,2048]{1,0:T(8,128)} fusion(bf16[1,2048,768]{2,1,0:T(8,128)(2,1)} %param.27, bf16[1,1024,768]{2,1,0:T(8,128)(2,1)} %all-gather.10.cloned.1.call-done, f32[1024]{0:T(1024)S(1)} %copy-done.66), kind=kOutput, calls=%fused_computation.29 | convolution fusion | flops 3223584768 | bytes 13111296 | tf_op jit(solution)/shard_map/dot_general | solution.py:23
  174.7 10.1 %multiply_convert_fusion.3 = (bf16[1024,2048]{1,0:T(8,128)(2,1)S(1)}, bf16[1024,2048]{1,0:T(8,128)(2,1)S(1)}, bf16[1024,2048]{1,0:T(8,128)(2,1)S(1)}) fusion(f32[1024,2048]{1,0:T(8,128)} %fusion.19, f32[1024,2048]{1,0:T(8,128)} %fusion.9, bf16[1024,768]{1,0:T(8,128)(2,1)S(1)} %copy-done.24, bf16[1,768,2048]{2,1,0:T(8,128)(2,1)S(1)} %copy-done), kind=kOutput, calls=%fused_computation.8 | convolution fusion | flops 3252682752 | bytes 34078720 | tf_op jit(solution)/shard_map/dot_general | solution.py:19
  184.8 3.5 fusion.13
  197.8 4.8 all-to-all-start
  214.1 59.4 %all-to-all-done = bf16[4,2,256,768]{3,2,1,0:T(8,128)(2,1)} async-done(((bf16[4,2,256,768]{3,2,1,0:T(8,128)(2,1)}), bf16[4,2,256,768]{3,2,1,0:T(8,128)(2,1)}, u32[]{:S(2)}, u32[]{:S(2)}) %all-to-all-start) | async-done | bytes 3145760 | tf_op jit(solution)/shard_map/all_to_all | solution.py:734
  281.6 6.3 %fusion.28 = bf16[12,64,1024]{2,1,0:T(8,128)(2,1)S(1)} fusion(bf16[256,12,64]{0,2,1:T(8,128)(2,1)S(1)} %bitcast.250, f32[12,256,1024]{2,1,0:T(8,128)} %get-tuple-element.132, f32[12,256]{1,0:T(8,128)} %copy-done.53), kind=kOutput, calls=%fused_computation.53 | convolution fusion | flops 409731072 | bytes 14561280 | tf_op jit(solution)/shard_map/hqk,qhd->khd/dot_general | solution.py:777
  287.9 9.1 %multiply_reduce_fusion = (f32[12,256]{1,0:T(8,128)S(1)}, f32[12,256,1024]{2,1,0:T(8,128)}) fusion(f32[12,256,1024]{2,1,0:T(8,128)} %get-tuple-element.132, f32[12,256]{1,0:T(8,128)S(1)} %copy-done.54, bf16[256,12,64]{0,2,1:T(8,128)(2,1)S(1)} %bitcast.251, bf16[1024,12,64]{0,2,1:T(8,128)(2,1)S(1)} %bitcast.244), kind=kOutput, calls=%fused_computation.2 | convolution fusion | flops 412087296 | bytes 27156480 | tf_op jit(solution)/shard_map/qhd,khd->hqk/dot_general | solution.py:766
  297.0 5.8 %multiply_convert_fusion = bf16[12,256,1024]{2,1,0:T(8,128)(2,1)S(1)} fusion(f32[12,256,1024]{2,1,0:T(8,128)} %get-tuple-element.141, f32[12,256]{1,0:T(8,128)S(1)} %get-tuple-element.140, f32[12,256,1024]{2,1,0:T(8,128)S(1)} %bitcast.222, f32[12,256]{1,0:T(8,128)S(1)} %copy-done.54), kind=kLoop, calls=%fused_computation.1 | loop fusion | flops 12582912 | bytes 31481856 | tf_op jit(solution)/shard_map/convert_element_type | solution.py:770
  308.1 4.0 convolution_convert_fusion.2
  318.9 4.8 convolution_convert_fusion.5
  323.7 4.8 convolution_convert_fusion.4
  328.7 5.6 %convolution_convert_fusion.3 = bf16[2048,768]{1,0:T(8,128)(2,1)} fusion(bf16[1024,2048]{1,0:T(8,128)(2,1)S(1)} %copy-done.81, bf16[1,1024,768]{2,1,0:T(8,128)(2,1)S(1)} %copy-done.75, f32[1024]{0:T(1024)S(1)} %copy-done.67), kind=kOutput, calls=%fused_computation.20 | convolution fusion | flops 3225157632 | bytes 8916992 | tf_op jit(solution)/shard_map/dot_general | solution.py:29
  340.5 4.2 reduce-scatter.2.cloned.1.call-done
  355.3 150.2 %reduce_grads.1 = (bf16[2,2,2,96,2048]{4,3,2,1,0:T(8,128)(2,1)}, bf16[2,2,2,96,2048]{4,3,2,1,0:T(8,128)(2,1)}, bf16[2,2,2,256,768]{4,3,2,1,0:T(8,128)(2,1)}, f32...) custom-call(bf16[2,2,2,96,2048]{4,3,2,1,0:T(8,128)(2,1)} %bitcast.23, ...), custom_call_target="tpu_custom_call" | custom-call | tf_op jit(solution)/shard_map/reduce_grads/pallas_call | solution.py:618
  506.9 5.6 %convert.38 = f32[1,768,2048]{2,1,0:T(8,128)} convert(bf16[1,768,2048]{2,1,0:T(8,128)(2,1)} %bitcast.240) | non-fusion elementwise | flops 1572864 | bytes 9437184 | tf_op jit(solution)/shard_map/convert_element_type | solution.py:822
  512.4 3.6 convert.39
  (268 shorter events, 109.2 us)
Async XLA Ops:
  7.2 167.5 %copy-start = (bf16[1,768,2048]{2,1,0:T(8,128)(2,1)S(1)}, bf16[1,768,2048]{2,1,0:T(8,128)(2,1)}, u32[]{:S(2)}) copy-start(bf16[1,768,2048]{2,1,0:T(8,128)(2,1)} %param.26) | copy-start | bytes 9437188
  7.2 53.1 %all-gather.6.cloned.1.call-start = ((), (), s32[]{:S(2)}) async-start(), calls=%async_computation.2 | async-start | bytes 3932160 | tf_op jit(solution)/shard_map/all_gather | solution.py:678
  10.1 10.2 %copy-start.41 = (f32[256]{0:T(256)}, f32[256]{0:T(256)S(1)}, u32[]{:S(2)}) copy-start(f32[256]{0:T(256)S(1)} %fusion.90) | copy-start | bytes 3076
  28.9 98.9 %all-gather.8.cloned.1.call-start = ((), (), s32[]{:S(2)}) async-start(), calls=%async_computation.3 | async-start | bytes 1966080 | tf_op jit(solution)/shard_map/all_gather | solution.py:711
  80.5 9.2 %copy-start.47 = (f32[768]{0:T(1024)S(1)}, f32[768]{0:T(1024)}, u32[]{:S(2)}) copy-start(f32[768]{0:T(1024)} %param.23) | copy-start | bytes 9220
  87.7 40.1 %copy-start.43 = (bf16[768,4]{0,1:T(4,128)(2,1)S(1)}, bf16[768,4]{0,1:T(4,128)(2,1)}, u32[]{:S(2)}) copy-start(bf16[768,4]{0,1:T(4,128)(2,1)} %param.24) | copy-start | bytes 18436
  90.6 74.8 %all-gather.10.cloned.1.call-start = ((), (), s32[]{:S(2)}) async-start(), calls=%async_computation.5 | async-start | bytes 1966080 | tf_op jit(solution)/shard_map/all_gather | solution.py:664
  131.1 34.2 %copy-start.66 = (f32[1024]{0:T(1024)S(1)}, f32[1024]{0:T(1024)}, u32[]{:S(2)}) copy-start(f32[1024]{0:T(1024)} %select_reduce_fusion) | copy-start | bytes 12292
  165.4 9.3 %copy-start.24 = (bf16[1024,768]{1,0:T(8,128)(2,1)S(1)}, bf16[1024,768]{1,0:T(8,128)(2,1)}, u32[]{:S(2)}) copy-start(bf16[1024,768]{1,0:T(8,128)(2,1)} %all-gather.8.cloned.1.call-done) | copy-start | bytes 4718596
  197.8 75.7 %all-to-all-start = ((bf16[4,2,256,768]{3,2,1,0:T(8,128)(2,1)}), bf16[4,2,256,768]{3,2,1,0:T(8,128)(2,1)}, u32[]{:S(2)}, u32[]{:S(2)}) async-start(bf16[4,2,256,768]{3,2,1,0:T(8,128)(2,1)} %pad_maximum_fusion), calls=%async_computation | async-start | bytes 6291456 | tf_op jit(solution)/shard_map/all_to_all | solution.py:734
  202.6 142.1 %reduce-scatter.2.cloned.1.call-start = ((), (), s32[]{:S(2)}) async-start(), calls=%async_computation.4 | async-start | bytes 3932160 | tf_op jit(solution)/shard_map/reduce_scatter | solution.py:781
  202.9 74.0 %copy-start.44 = (pred[256,4]{0,1:T(4,128)(4,1)}, pred[256,4]{0,1:T(4,128)(4,1)S(1)}, u32[]{:S(2)}) copy-start(pred[256,4]{0,1:T(4,128)(4,1)S(1)} %fusion.78) | copy-start | bytes 3076
  203.2 73.6 %copy-start.49 = (f32[256]{0:T(256)}, f32[256]{0:T(256)S(1)}, u32[]{:S(2)}) copy-start(f32[256]{0:T(256)S(1)} %get-tuple-element.137) | copy-start | bytes 3076
  203.3 73.6 %copy-start.51 = (f32[256]{0:T(256)}, f32[256]{0:T(256)S(1)}, u32[]{:S(2)}) copy-start(f32[256]{0:T(256)S(1)} %fusion.87) | copy-start | bytes 3076
  214.1 64.5 %copy-start.6 = (f32[256,768]{1,0:T(8,128)S(1)}, f32[256,768]{1,0:T(8,128)}, u32[]{:S(2)}) copy-start(f32[256,768]{1,0:T(8,128)} %copy-done.5) | copy-start | bytes 2359300
  281.6 15.4 %slice-start.2 = ((s8[12582912]{0:T(1024)(128)(4,1)}), s8[4194304]{0:T(1024)(128)(4,1)S(1)}, s32[]{:S(2)}) async-start(s8[12582912]{0:T(1024)(128)(4,1)} %bitcast.221), calls=%async_computation.8 | async-start | bytes 8388608
  281.6 15.4 %slice-start.3 = ((s8[12582912]{0:T(1024)(128)(4,1)}), s8[4194304]{0:T(1024)(128)(4,1)S(1)}, s32[]{:S(2)}) async-start(s8[12582912]{0:T(1024)(128)(4,1)} %bitcast.221), calls=%async_computation.9 | async-start | bytes 8388608
  287.9 9.1 %slice-start.4 = ((s8[12582912]{0:T(1024)(128)(4,1)}), s8[4194304]{0:T(1024)(128)(4,1)S(1)}, s32[]{:S(2)}) async-start(s8[12582912]{0:T(1024)(128)(4,1)} %bitcast.221), calls=%async_computation.10 | async-start | bytes 8388608
  323.7 14.8 %slice-start = ((s8[6291456]{0:T(1024)(128)(4,1)}), s8[4194304]{0:T(1024)(128)(4,1)S(1)}, s32[]{:S(2)}) async-start(s8[6291456]{0:T(1024)(128)(4,1)} %bitcast.215), calls=%async_computation.6 | async-start | bytes 8388608
  328.6 8.0 %copy-start.33 = (f32[256,768]{1,0:T(8,128)S(1)}, f32[256,768]{1,0:T(8,128)}, u32[]{:S(2)}) copy-start(f32[256,768]{1,0:T(8,128)} %get-tuple-element.98) | copy-start | bytes 2359300
  328.6 9.8 %slice-start.1 = ((s8[6291456]{0:T(1024)(128)(4,1)}), s8[2097152]{0:T(1024)(128)(4,1)S(1)}, s32[]{:S(2)}) async-start(s8[6291456]{0:T(1024)(128)(4,1)} %bitcast.215), calls=%async_computation.7 | async-start | bytes 4194304
  516.0 14.5 %copy-start.1 = (bf16[1,768,2048]{2,1,0:T(8,128)(2,1)S(1)}, bf16[1,768,2048]{2,1,0:T(8,128)(2,1)}, u32[]{:S(2)}) copy-start(bf16[1,768,2048]{2,1,0:T(8,128)(2,1)} %param.26) | copy-start | bytes 9437188
  520.9 8.2 %copy-start.38 = (f32[96,512]{1,0:T(8,128)S(1)}, f32[96,512]{1,0:T(8,128)}, u32[]{:S(2)}) copy-start(f32[96,512]{1,0:T(8,128)} %get-tuple-element.172) | copy-start | bytes 589828
  520.9 8.9 %copy-start.37 = (f32[96,512]{1,0:T(8,128)S(1)}, f32[96,512]{1,0:T(8,128)}, u32[]{:S(2)}) copy-start(f32[96,512]{1,0:T(8,128)} %get-tuple-element.173) | copy-start | bytes 589828
  (68 other events, 277.4 us)
Sparse Core Ops, SparseCore 0:
  29.0 31.2 all-gather.5
  90.7 37.1 all-gather.7
  129.4 35.9 all-gather.9
  307.6 36.9 reduce-scatter.1

commit v3 on v0

--- a/solution.py
+++ b/solution.py
@@ -1,14 +1,19 @@
+import functools
 import math
 
 import jax
 import jax.numpy as jnp
+import numpy as np
 from jax import lax
+from jax.experimental import pallas as pl
+from jax.experimental.pallas import tpu as pltpu
 from jax.sharding import PartitionSpec as P
 
 HEAD_DIM = 64
 TOP = 2
 BLOCK = 256
 KEY_ROWS = 512
+MESH = pl.DeviceIdType.MESH
 
 
 def product(first_factor, second_factor):
@@ -57,7 +62,7 @@
     return blocks.reshape(col_groups * row_count, col_count // col_groups)
 
 
-def per_device(
+def per_device_slots(
     tokens,
     expert_ids,
     norm_one,
@@ -172,7 +177,10 @@
     slot_hits = (flat_ids[:, None] == jnp.arange(experts_all, dtype=jnp.int32)[None, :]).astype(
         jnp.int32
     )
-    slot_place = jnp.sum((jnp.cumsum(slot_hits, axis=0) - slot_hits) * slot_hits, axis=1)
+    order = jnp.arange(flat_ids.shape[0], dtype=jnp.int32)
+    earlier = (order[None, :] < order[:, None]).astype(jnp.bfloat16)
+    counts_before = product(earlier, slot_hits.astype(jnp.bfloat16)).astype(jnp.int32)
+    slot_place = jnp.sum(counts_before * slot_hits, axis=1)
 
     def to_slots(routed_rows):
         empty_slots = jnp.zeros((experts_all, capacity, model_width), jnp.bfloat16)
@@ -403,7 +411,829 @@
     )
 
 
+def place_tables(length):
+    half = HEAD_DIM // 2
+    frequency = np.float32(10000.0) ** (-np.arange(half, dtype=np.float32) / np.float32(half))
+    angles = np.arange(length, dtype=np.float32)[:, None] * frequency[None, :].astype(np.float32)
+    cosine, sine = np.cos(angles), np.sin(angles)
+    return (
+        np.concatenate([cosine] * 4, axis=1).astype(np.float32),
+        np.concatenate([-sine, sine, -sine, sine], axis=1).astype(np.float32),
+    )
+
+
+def swapped(values):
+    half = HEAD_DIM // 2
+    lane = lax.broadcasted_iota(jnp.int32, values.shape, 1) % HEAD_DIM
+    return jnp.where(lane < half, pltpu.roll(values, 128 - half, 1), pltpu.roll(values, half, 1))
+
+
+def start_copy(src, dst, ssem, rsem, device):
+    copy = pltpu.make_async_remote_copy(
+        src_ref=src, dst_ref=dst, send_sem=ssem, recv_sem=rsem, device_id=device, device_id_type=MESH
+    )
+    copy.start()
+    return copy
+
+
+def greet(devices):
+    barrier = pltpu.get_barrier_semaphore()
+    for device in devices:
+        pl.semaphore_signal(barrier, inc=1, device_id=device, device_id_type=MESH)
+    pl.semaphore_wait(barrier, len(devices))
+
+
+def neighbours():
+    s = lax.axis_index("seq")
+    c = lax.axis_index("ctx")
+    e = lax.axis_index("exp")
+    x, k = c // 2, c % 2
+    to_core = (s, x * 2 + (1 - k), e)
+    to_x = (s, (1 - x) * 2 + k, e)
+    to_y = (1 - s, c, e)
+    near = e + 1 - 2 * (e % 2)
+    far = lax.rem(e + 2, 4)
+    opposite = 3 - e
+    return s, x, k, e, c, to_core, to_x, to_y, (near, far, opposite)
+
+
+def front_kernel(
+    tokens, upstream, named, gain_one, gain_two, w_q, w_k, w_v, w_o, cosine, sine,
+    q_all, k_all, v_all, upstream_all, named_all, normed_out, attended_out, mixed_out, second_out, logsum_out,
+    block, tsem, trem, usem, urem, nsem, nrem,
+):
+    s, x, k, e, c, to_core, to_x, to_y, others = neighbours()
+    rows, width = tokens.shape
+    greet([to_core, to_x, *[(s, c, o) for o in others]])
+    block[c] = tokens[...]
+    upstream_all[0] = upstream[...]
+    named_all[0] = named[...]
+    core_copy = start_copy(tokens, block.at[c], tsem.at[0], trem.at[0], to_core)
+    x_copy = start_copy(tokens, block.at[c], tsem.at[1], trem.at[1], to_x)
+    z_copies = []
+    for i in range(3):
+        device = (s, c, others[i])
+        z_copies.append(start_copy(named, named_all.at[i + 1], nsem.at[i], nrem.at[i], device))
+        z_copies.append(start_copy(upstream, upstream_all.at[i + 1], usem.at[i], urem.at[i], device))
+
+    def project(j):
+        values = block[j].astype(jnp.float32)
+        inverse = lax.rsqrt(jnp.mean(values * values, axis=-1, keepdims=True) + 1e-06)
+        normed = (values * inverse * gain_one[...]).astype(jnp.bfloat16)
+        for weight, out in ((w_q, q_all), (w_k, k_all)):
+            lin = jnp.dot(normed, weight[...], preferred_element_type=jnp.float32)
+            for g in range(width // 128):
+                part = lin[:, g * 128 : (g + 1) * 128]
+                turned = part * cosine[j] + swapped(part) * sine[j]
+                out[j, :, g * 128 : (g + 1) * 128] = turned.astype(jnp.bfloat16)
+        v_all[j] = jnp.dot(normed, w_v[...], preferred_element_type=jnp.float32).astype(jnp.bfloat16)
+        return normed
+
+    normed_out[...] = project(c)
+    core_copy.wait()
+    project(x * 2 + (1 - k))
+    x_copy.wait()
+    there = (1 - x) * 2 + k
+    corner_copy = start_copy(block.at[there], block.at[there], tsem.at[2], trem.at[2], to_core)
+    project(there)
+    corner_copy.wait()
+    project((1 - x) * 2 + (1 - k))
+
+    span = 4 * rows
+    hidden_keys = lax.broadcasted_iota(jnp.int32, (1, span), 1) // rows > c
+    bias = jnp.where(hidden_keys, -1e30, 0.0)
+    lane = lax.broadcasted_iota(jnp.int32, (rows, 128), 1)
+    logsum_out[...] = jnp.zeros_like(logsum_out)
+
+    def pair(g, carry):
+        at = pl.ds(pl.multiple_of(g * 128, 128), 128)
+        q = q_all[c, :, at]
+        keys = k_all[:, :, at].reshape(span, 128)
+        values = v_all[:, :, at].reshape(span, 128)
+        out = jnp.zeros((rows, 128), jnp.float32)
+        for h in range(2):
+            inside = (lane // HEAD_DIM) == h
+            scores = lax.dot_general(
+                jnp.where(inside, q, jnp.zeros_like(q)), keys, (((1,), (1,)), ((), ())),
+                preferred_element_type=jnp.float32,
+            )
+            scores = scores * (HEAD_DIM**-0.5) + bias
+            highest = jnp.max(scores, axis=-1, keepdims=True)
+            raised = jnp.exp(scores - highest)
+            total = jnp.sum(raised, axis=-1, keepdims=True)
+            mixed = jnp.dot(raised.astype(jnp.bfloat16), values, preferred_element_type=jnp.float32)
+            out = jnp.where(inside, mixed / total, out)
+            logsum_out[...] = jnp.where(lane == 2 * g + h, highest + jnp.log(total), logsum_out[...])
+        attended_out[:, at] = out.astype(jnp.bfloat16)
+        return carry
+
+    lax.fori_loop(0, width // 128, pair, 0)
+    mixed = tokens[...].astype(jnp.float32) + jnp.dot(
+        attended_out[...], w_o[...], preferred_element_type=jnp.float32
+    )
+    mixed_out[...] = mixed
+    inverse = lax.rsqrt(jnp.mean(mixed * mixed, axis=-1, keepdims=True) + 1e-06)
+    second_out[...] = (mixed * inverse * gain_two[...]).astype(jnp.bfloat16)
+    for copy in z_copies:
+        copy.wait()
+
+
+def front(tokens, upstream, named, gain_one, gain_two, w_q, w_k, w_v, w_o):
+    rows, width = tokens.shape
+    cosine, sine = (jnp.asarray(t).reshape(4, rows, 128) for t in place_tables(4 * rows))
+    low, full = jnp.bfloat16, jnp.float32
+    vmem, dma = pltpu.VMEM, pltpu.SemaphoreType.DMA
+    every = jax.ShapeDtypeStruct((4, rows, width), low)
+    own = jax.ShapeDtypeStruct((rows, width), low)
+    spec = pl.BlockSpec(memory_space=pltpu.VMEM)
+    out_shape = [
+        every, every, every, every, jax.ShapeDtypeStruct((4, rows, 128), low), own, own,
+        jax.ShapeDtypeStruct((rows, width), full), own, jax.ShapeDtypeStruct((rows, 128), full),
+    ]
+    return pl.pallas_call(
+        front_kernel,
+        out_shape=out_shape,
+        in_specs=[spec] * 11,
+        out_specs=[spec] * 10,
+        scratch_shapes=[vmem((4, rows, width), low), dma((3,)), dma((3,)), dma((3,)), dma((3,)), dma((3,)), dma((3,))],
+        compiler_params=pltpu.CompilerParams(
+            collective_id=2, has_side_effects=True, vmem_limit_bytes=58 * 2**20
+        ),
+        name="front",
+    )(tokens, upstream, named, gain_one.reshape(1, width), gain_two.reshape(1, width), w_q, w_k, w_v, w_o, cosine, sine)
+
+
+def add_rows(target, first, second, step):
+    rows = target.shape[0]
+
+    def some(at):
+        total = first[at, :].astype(jnp.float32) + second[at, :].astype(jnp.float32)
+        target[at, :] = total.astype(target.dtype)
+
+    if rows <= step:
+        some(pl.ds(0, rows))
+    else:
+
+        def body(i, carry):
+            some(pl.ds(pl.multiple_of(i * step, step), step))
+            return carry
+
+        lax.fori_loop(0, rows // step, body, 0)
+
+
+class Piece:
+    def __init__(self, place, whole, one, two, three, half, sems, step):
+        self.s, self.x, self.k, self.to_core, self.to_x, self.to_y = place
+        self.whole, self.one, self.two, self.three = whole, one, two, three
+        self.half, self.sems, self.step = half, sems, step
+
+    def copy(self, level, h=0):
+        every, low, high = slice(None), pl.ds(0, self.half), pl.ds(self.half, self.half)
+        if level == 1:
+            src, dst, device = self.whole(1 - self.k), self.one(every, every, every), self.to_core
+        elif level == 2:
+            if h == 0:
+                src, device = self.one(every, 1 - self.x, low), self.to_x
+            else:
+                src, device = self.one(1 - self.s, every, high), self.to_y
+            dst = self.two(h, every)
+        else:
+            src = self.two(h, 1 - (self.s, self.x)[h])
+            dst, device = self.three(h), (self.to_y, self.to_x)[h]
+        ssem, rsem = self.sems(2 * (level - 1) - (1 if level > 1 else 0) + h)
+        return pltpu.make_async_remote_copy(
+            src_ref=src, dst_ref=dst, send_sem=ssem, recv_sem=rsem, device_id=device, device_id_type=MESH
+        )
+
+    def start(self, level):
+        for h in range(1 if level == 1 else 2):
+            self.copy(level, h).start()
+
+    def finish(self, level):
+        low, high = pl.ds(0, self.half), pl.ds(self.half, self.half)
+        if level == 1:
+            self.copy(1).wait()
+            own = self.whole(self.k)
+            for i in range(2):
+                for j in range(2):
+                    here = self.one(i, j, slice(None))
+                    add_rows(here, here, own.at[i, j], self.step)
+            return
+        for h in range(2):
+            self.copy(level, h).wait()
+            if level == 2:
+                for i in range(2):
+                    here = self.two(h, i)
+                    own = self.one(i, self.x, low) if h == 0 else self.one(self.s, i, high)
+                    add_rows(here, here, own, self.step)
+            else:
+                here = self.three(h)
+                add_rows(here, here, self.two(h, (self.s, self.x)[h]), self.step)
+
+
+def gates_in(logits, named):
+    masked = jnp.where(named, logits, -1e30)
+    raised = jnp.where(named, jnp.exp(masked - jnp.max(masked, axis=-1, keepdims=True)), 0.0)
+    return raised / jnp.sum(raised, axis=-1, keepdims=True)
+
+
+def ffn_kernel(
+    second, mixed, upstream_all, named_all, w_r, gain_two,
+    e_gate, e_up, e_down, s_gate, s_up, s_down,
+    results, shares_out, base_out, d_mixed_out, small_out, eg_out, eu_out, ed_out, sg_out, su_out, sd_out,
+    rows_all, d_res, res_acc, row_acc, row_send, row_got, dg_send, dg_got, d_second,
+    t_gate, t_up, t_down, wsem,
+    ge_g, ge_u, ge_d, e1_g, e1_u, e1_d, e2_g, e2_u, e2_d,
+    gs_g, gs_u, gs_d, s1_g, s1_u, s1_d, s2_g, s2_u, s2_d,
+    es_sem, er_sem, ss_sem, sr_sem, xs_sem, xr_sem, rs_sem, rr_sem, ds_sem, dr_sem,
+):
+    s, x, k, e, c, to_core, to_x, to_y, others = neighbours()
+    place = (s, x, k, to_core, to_x, to_y)
+    rows, width = second.shape
+    tile = t_gate.shape[2]
+    tiles = e_gate.shape[1] // tile
+    low, full = jnp.bfloat16, jnp.float32
+    greet([to_core, to_x, to_y, *[(s, c, o) for o in others]])
+    rows_all[0] = second[...]
+    row_copies = [
+        start_copy(second, rows_all.at[i + 1], xs_sem.at[i], xr_sem.at[i], (s, c, others[i])) for i in range(3)
+    ]
+
+    def columns(f):
+        return pl.ds(pl.multiple_of(f * tile, tile), tile)
+
+    def fetches(sources, f, slot):
+        gate, up, down = sources
+        return [
+            pltpu.make_async_copy(gate.at[:, columns(f)], t_gate.at[slot], wsem.at[slot, 0]),
+            pltpu.make_async_copy(up.at[:, columns(f)], t_up.at[slot], wsem.at[slot, 1]),
+            pltpu.make_async_copy(down.at[columns(f), :], t_down.at[slot], wsem.at[slot, 2]),
+        ]
+
+    def next_tile(sources, following, f):
+        slot = lax.rem(f, 2)
+
+        @pl.when(f < tiles - 1)
+        def _():
+            for copy in fetches(sources, f + 1, 1 - slot):
+                copy.start()
+
+        if following is not None:
+
+            @pl.when(f == tiles - 1)
+            def _():
+                for copy in fetches(following, 0, 1 - slot):
+                    copy.start()
+
+        for copy in fetches(sources, f, slot):
+            copy.wait()
+        return slot
+
+    def piece_e(f, a):
+        at = columns(f)
+        sems = lambda n: (es_sem.at[f, a, n], er_sem.at[f, a, n])
+        if a < 2:
+            g, one, two, three = ((ge_g, e1_g, e2_g, eg_out), (ge_u, e1_u, e2_u, eu_out))[a]
+            return Piece(
+                place,
+                lambda kk: g.at[:, :, kk, :, at],
+                lambda i, j, r: one.at[i, j, r, at],
+                lambda h, i: two.at[h, i, :, at],
+                lambda h: three.at[h, :, at],
+                g.shape[3] // 2, sems, 96,
+            )
+        return Piece(
+            place,
+            lambda kk: ge_d.at[f, :, :, kk],
+            lambda i, j, r: e1_d.at[f, i, j, r],
+            lambda h, i: e2_d.at[f, h, i],
+            lambda h: ed_out.at[f, h],
+            ge_d.shape[4] // 2, sems, 96,
+        )
+
+    def piece_s(a):
+        g, one, two, three = (
+            (gs_g, s1_g, s2_g, sg_out), (gs_u, s1_u, s2_u, su_out), (gs_d, s1_d, s2_d, sd_out)
+        )[a]
+        return Piece(
+            place,
+            lambda kk: g.at[:, :, kk],
+            lambda i, j, r: one.at[i, j, r],
+            lambda h, i: two.at[h, i],
+            lambda h: three.at[h],
+            g.shape[3] // 2, lambda n: (ss_sem.at[a, n], sr_sem.at[a, n]), 16 if a < 2 else 32,
+        )
+
+    shared, expert = (s_gate, s_up, s_down), (e_gate, e_up, e_down)
+    for copy in fetches(shared, 0, 0):
+        copy.start()
+
+    def branch(values, d_out, slot, result_acc, d_acc):
+        gate_w, up_w, down_w = t_gate[slot], t_up[slot], t_down[slot]
+        gate = jnp.dot(values, gate_w, preferred_element_type=full)
+        up = jnp.dot(values, up_w, preferred_element_type=full)
+        d_hidden = against(d_out, down_w)
+        sigmoid = 1.0 / (1.0 + jnp.exp(-gate))
+        silu = gate * sigmoid
+        hidden = (silu * up).astype(low)
+        d_gate = (d_hidden * up * (sigmoid * (1.0 + gate * (1.0 - sigmoid)))).astype(low)
+        d_up = (d_hidden * silu).astype(low)
+        result_acc[...] += jnp.dot(hidden, down_w, preferred_element_type=full)
+        d_acc[...] += against(d_gate, gate_w) + against(d_up, up_w)
+        return hidden, d_gate, d_up
+
+    base_out[...] = mixed[...]
+    d_second[...] = jnp.zeros_like(d_second)
+
+    def shared_tile(f, carry):
+        slot = next_tile(shared, expert, f)
+        values, d_out = second[...], upstream_all[0]
+        hidden, d_gate, d_up = branch(values, d_out, slot, base_out, d_second)
+        gs_g[:, :, :, :, columns(f)] = outer_sum(values, d_gate).astype(low).reshape(2, 2, 2, width // 8, tile)
+        gs_u[:, :, :, :, columns(f)] = outer_sum(values, d_up).astype(low).reshape(2, 2, 2, width // 8, tile)
+        gs_d[f // 4, (f // 2) % 2, f % 2] = outer_sum(hidden, d_out).astype(low)
+        return carry
+
+    lax.fori_loop(0, tiles, shared_tile, 0)
+    for a in range(3):
+        piece_s(a).start(1)
+    logits = jnp.dot(second[...], w_r[...], preferred_element_type=full)
+    shares_out[...] = gates_in(logits, named_all[0].astype(full) > 0.5)
+
+    lane = lax.broadcasted_iota(jnp.int32, (2 * rows, 128), 1)
+    for turn in range(2):
+        if turn == 0:
+            row_copies[0].wait()
+        else:
+            row_copies[1].wait()
+            row_copies[2].wait()
+        pair = pl.ds(2 * turn, 2)
+        values = rows_all[pair].reshape(2 * rows, width)
+        logits = jnp.dot(values, w_r[...], preferred_element_type=full)
+        gates = gates_in(logits, named_all[pair].reshape(2 * rows, 128).astype(full) > 0.5)
+        share = jnp.sum(jnp.where(lane == e, gates, 0.0), axis=-1, keepdims=True)
+        d_res[...] = (share * upstream_all[pair].reshape(2 * rows, width).astype(full)).astype(low)
+        res_acc[...] = jnp.zeros_like(res_acc)
+        row_acc[...] = jnp.zeros_like(row_acc)
+
+        def expert_tile(f, carry, turn=turn, pair=pair):
+            slot = next_tile(expert, expert if turn == 0 else None, f)
+            values, d_out = rows_all[pair].reshape(2 * rows, width), d_res[...]
+            hidden, d_gate, d_up = branch(values, d_out, slot, res_acc, row_acc)
+            for g, term in ((ge_g, outer_sum(values, d_gate)), (ge_u, outer_sum(values, d_up))):
+                term = term.reshape(2, 2, 2, width // 8, tile)
+                if turn == 1:
+                    term = term + g[:, :, :, :, columns(f)].astype(full)
+                g[:, :, :, :, columns(f)] = term.astype(low)
+            term = outer_sum(hidden, d_out).reshape(2, 2, 2, tile // 8, width)
+            if turn == 1:
+                term = term + ge_d[f].astype(full)
+            ge_d[f] = term.astype(low)
+            if turn == 0:
+                for a in range(3):
+
+                    @pl.when(f == 2 * a + 2)
+                    def _(a=a):
+                        piece_s(a).finish(1)
+                        piece_s(a).start(2)
+
+            else:
+                for a in range(3):
+                    piece_e(f, a).start(1)
+
+                @pl.when(f > 0)
+                def _():
+                    for a in range(3):
+                        piece_e(f - 1, a).finish(1)
+                        piece_e(f - 1, a).start(2)
+
+            return carry
+
+        lax.fori_loop(0, tiles, expert_tile, 0)
+        low_result = res_acc[...].astype(low)
+        results[pair] = low_result.reshape(2, rows, width)
+        row_send[pair] = row_acc[...].astype(low).reshape(2, rows, width)
+        terms = low_result.astype(full) * upstream_all[pair].reshape(2 * rows, width).astype(full)
+        high = terms.astype(low)
+        ones = jnp.ones((8, width), low)
+        sums = against(ones, high) + against(ones, (terms - high.astype(full)).astype(low))
+        for i in range(2):
+            dg_send[2 * turn + i] = sums[:, i * rows : (i + 1) * rows]
+        for i in (1,) if turn == 0 else (2, 3):
+            device = (s, c, others[i - 1])
+            start_copy(row_send.at[i], row_got.at[i], rs_sem.at[i], rr_sem.at[i], device)
+            start_copy(dg_send.at[i], dg_got.at[i], ds_sem.at[i], dr_sem.at[i], device)
+
+    for a in range(3):
+        piece_e(tiles - 1, a).finish(1)
+        piece_e(tiles - 1, a).start(2)
+    for a in range(3):
+        piece_s(a).finish(2)
+        piece_s(a).start(3)
+
+    def third(f, carry):
+        for a in range(3):
+            piece_e(f, a).finish(2)
+            piece_e(f, a).start(3)
+        return carry
+
+    lax.fori_loop(0, tiles, third, 0)
+
+    d_gates = jnp.where(lax.broadcasted_iota(jnp.int32, (8, rows), 0) == e, dg_send[0], 0.0)
+    total = d_second[...] + row_send[0].astype(full)
+    for i in range(1, 4):
+        device = (s, c, others[i - 1])
+        pltpu.make_async_remote_copy(
+            src_ref=row_send.at[i], dst_ref=row_got.at[i], send_sem=rs_sem.at[i], recv_sem=rr_sem.at[i],
+            device_id=device, device_id_type=MESH,
+        ).wait()
+        pltpu.make_async_remote_copy(
+            src_ref=dg_send.at[i], dst_ref=dg_got.at[i], send_sem=ds_sem.at[i], recv_sem=dr_sem.at[i],
+            device_id=device, device_id_type=MESH,
+        ).wait()
+        d_gates = jnp.where(
+            lax.broadcasted_iota(jnp.int32, (8, rows), 0) == others[i - 1], dg_got[i], d_gates
+        )
+        total = total + row_got[i].astype(full)
+    d_gates = jnp.concatenate([d_gates, jnp.zeros((120, rows), full)], axis=0).T
+    shares = shares_out[...]
+    d_logits = (shares * (d_gates - jnp.sum(shares * d_gates, axis=-1, keepdims=True))).astype(low)
+    total = total + against(d_logits, w_r[...])
+    router = outer_sum(d_logits, second[...])
+    values = mixed[...]
+    inverse = lax.rsqrt(jnp.mean(values * values, axis=-1, keepdims=True) + 1e-06)
+    unit = values * inverse
+    small_out[0:8, :] = router[0:8, :]
+    small_out[8:16, :] = jnp.broadcast_to(jnp.sum(total * unit, axis=0, keepdims=True), (8, width))
+    inner = total * gain_two[...]
+    mean = jnp.mean(inner * unit, axis=-1, keepdims=True)
+    d_mixed_out[...] = upstream_all[0].astype(full) + inverse * (inner - unit * mean)
+
+    for a in range(3):
+        piece_s(a).finish(3)
+
+    def done(f, carry):
+        for a in range(3):
+            piece_e(f, a).finish(3)
+        return carry
+
+    lax.fori_loop(0, tiles, done, 0)
+
+
+def ffn(second, mixed, upstream_all, named_all, w_router, gain_two, experts, shared):
+    rows, width = second.shape
+    hidden = experts[0].shape[1]
+    tile = 256
+    tiles = hidden // tile
+    low, full = jnp.bfloat16, jnp.float32
+    dma = pltpu.SemaphoreType.DMA
+    ninth, small, tall = width // 8, tile // 8, hidden // 8
+
+    def vm(*shape, dtype=low):
+        return pltpu.VMEM(shape, dtype)
+
+    def out(*shape, dtype=low):
+        return jax.ShapeDtypeStruct(shape, dtype)
+
+    w_r = jnp.pad(w_router, ((0, 0), (0, 128 - w_router.shape[1])))
+    spec = pl.BlockSpec(memory_space=pltpu.VMEM)
+    out_shape = [
+        out(4, rows, width), out(rows, 128, dtype=full), out(rows, width, dtype=full), out(rows, width, dtype=full),
+        out(16, width, dtype=full), out(2, ninth // 2, hidden), out(2, ninth // 2, hidden),
+        out(tiles, 2, small // 2, width), out(2, ninth // 2, hidden), out(2, ninth // 2, hidden), out(2, tall // 2, width),
+    ]
+    scratch = [
+        vm(4, rows, width), vm(2 * rows, width), vm(2 * rows, width, dtype=full), vm(2 * rows, width, dtype=full),
+        vm(4, rows, width), vm(4, rows, width), vm(4, 8, rows, dtype=full), vm(4, 8, rows, dtype=full),
+        vm(rows, width, dtype=full),
+        vm(2, width, tile), vm(2, width, tile), vm(2, tile, width), dma((2, 3)),
+        vm(2, 2, 2, ninth, hidden), vm(2, 2, 2, ninth, hidden), vm(tiles, 2, 2, 2, small, width),
+        vm(2, 2, ninth, hidden), vm(2, 2, ninth, hidden), vm(tiles, 2, 2, small, width),
+        vm(2, 2, ninth // 2, hidden), vm(2, 2, ninth // 2, hidden), vm(tiles, 2, 2, small // 2, width),
+        vm(2, 2, 2, ninth, hidden), vm(2, 2, 2, ninth, hidden), vm(2, 2, 2, tall, width),
+        vm(2, 2, ninth, hidden), vm(2, 2, ninth, hidden), vm(2, 2, tall, width),
+        vm(2, 2, ninth // 2, hidden), vm(2, 2, ninth // 2, hidden), vm(2, 2, tall // 2, width),
+        dma((tiles, 3, 5)), dma((tiles, 3, 5)), dma((3, 5)), dma((3, 5)), dma((3,)), dma((3,)),
+        dma((4,)), dma((4,)), dma((4,)), dma((4,)),
+    ]
+    return pl.pallas_call(
+        ffn_kernel,
+        out_shape=out_shape,
+        in_specs=[spec] * 6 + [pl.BlockSpec(memory_space=pl.ANY)] * 6,
+        out_specs=[spec] * len(out_shape),
+        scratch_shapes=scratch,
+        compiler_params=pltpu.CompilerParams(
+            collective_id=3, has_side_effects=True, vmem_limit_bytes=60 * 2**20
+        ),
+        name="ffn",
+    )(second, mixed, upstream_all, named_all, w_r, gain_two.reshape(1, width), *experts, *shared)
+
+
+def close_kernel(
+    eg_own, eu_own, ed_own, sg_own, su_own, sd_own, gq, gk, gv, go, misc_in, results, base, shares,
+    eg_all, eu_all, ed_all, sg_out, su_out, sd_out, q_out, k_out, v_out, o_out, misc_out, output,
+    one, two, three, z_flat, z_tall, z_wide, got_flat, got_tall, got_wide, misc_got, result_got,
+    lsem, gsem, grem, psem, prem, zsem, zrem, msem, mrem, rsem, rrem,
+):
+    s, x, k, e, c, to_core, to_x, to_y, others = neighbours()
+    place = (s, x, k, to_core, to_x, to_y)
+    to_z = [(s, c, o) for o in others]
+    low, full = jnp.bfloat16, jnp.float32
+    greet([to_core, to_x, to_y, *to_z])
+
+    def piece(a):
+        g = (gq, gk, gv, go)[a]
+        return Piece(
+            place,
+            lambda kk: g.at[:, :, kk],
+            lambda i, j, r: one.at[a, i, j, r],
+            lambda h, i: two.at[a, h, i],
+            lambda h: three.at[a, h],
+            g.shape[3] // 2, lambda n: (psem.at[a, n], prem.at[a, n]), 48,
+        )
+
+    for a in range(4):
+        piece(a).start(1)
+    misc_copy = start_copy(misc_in, misc_got.at[0], msem.at[0], mrem.at[0], to_core)
+    result_copies = [
+        start_copy(results.at[i + 1], result_got.at[i], rsem.at[i], rrem.at[i], to_z[i]) for i in range(3)
+    ]
+
+    def block(a, h, ss, xx):
+        whole = (eg_all, eu_all, ed_all)[a]
+        half = whole.shape[-2] // 2
+        part = pl.ds(h * half, half)
+        return whole.at[ss, xx, k, part] if a < 2 else whole.at[:, ss, xx, k, part]
+
+    legs = []
+    for a, own in enumerate((eg_own, eu_own, ed_own)):
+        for h in range(2):
+            src = own.at[h] if a < 2 else own.at[:, h]
+            here = block(a, h, s, x)
+            local = pltpu.make_async_copy(src, here, lsem.at[a, h])
+            local.start()
+            near, wide = (to_y, to_x) if h == 0 else (to_x, to_y)
+            legs.append(
+                (
+                    local,
+                    start_copy(src, here, gsem.at[a, h, 0], grem.at[a, h, 0], near),
+                    start_copy(src, here, gsem.at[a, h, 1], grem.at[a, h, 1], wide),
+                )
+            )
+
+    def spread(own, buffer):
+        halves, height, across = own.shape
+        piece_width = across // 4
+        for h in range(halves):
+            for q in range(4):
+                buffer[q, pl.ds(h * height, height), :] = own[h, :, q * piece_width : (q + 1) * piece_width]
+
+    def to_owners(buffer, got, number):
+        owners = (e, *others)
+        return [
+            start_copy(buffer.at[owners[i]], got.at[i - 1], zsem.at[number, i - 1], zrem.at[number, i - 1], to_z[i - 1])
+            for i in range(1, 4)
+        ]
+
+    def settle(copies, buffer, got, target):
+        for copy in copies:
+            copy.wait()
+        target[...] = (
+            buffer[e].astype(full) + got[0].astype(full) + got[1].astype(full) + got[2].astype(full)
+        )
+
+    z_copies = []
+    for number, (own, buffer, got) in enumerate(
+        ((sg_own, z_wide.at[0], got_wide.at[0]), (su_own, z_wide.at[1], got_wide.at[1]), (sd_own, z_tall, got_tall))
+    ):
+        spread(own, buffer)
+        z_copies.append(to_owners(buffer, got, number))
+    for a in range(4):
+        piece(a).finish(1)
+        piece(a).start(2)
+    misc_copy.wait()
+    misc_out[...] = misc_in[...] + misc_got[0]
+    misc_copy = start_copy(misc_out, misc_got.at[1], msem.at[1], mrem.at[1], to_x)
+    onward = []
+    for a in range(3):
+        for h in range(2):
+            legs[2 * a + h][1].wait()
+            there = block(a, h, (1 - s, s)[h], (x, 1 - x)[h])
+            onward.append(start_copy(there, there, gsem.at[a, h, 2], grem.at[a, h, 2], (to_x, to_y)[h]))
+    for a in range(4):
+        piece(a).finish(2)
+        piece(a).start(3)
+    misc_copy.wait()
+    misc_got[3] = misc_out[...] + misc_got[1]
+    misc_copy = start_copy(misc_got.at[3], misc_got.at[2], msem.at[2], mrem.at[2], to_y)
+    for a in range(4):
+        piece(a).finish(3)
+        spread(three.at[a], z_flat.at[a])
+        z_copies.append(to_owners(z_flat.at[a], got_flat.at[a], 3 + a))
+    misc_copy.wait()
+    misc_got[4] = misc_got[3] + misc_got[2]
+    misc_copies = [
+        start_copy(misc_got.at[4], misc_got.at[5 + i], msem.at[3 + i], mrem.at[3 + i], to_z[i]) for i in range(3)
+    ]
+    last = []
+    for a, whole in enumerate((eg_all, eu_all, ed_all)):
+        for h in range(2):
+            legs[2 * a + h][0].wait()
+            legs[2 * a + h][2].wait()
+            onward[2 * a + h].wait()
+        there = whole.at[:, :, k] if a < 2 else whole.at[:, :, :, k]
+        last.append(start_copy(there, there, gsem.at[a, 0, 3], grem.at[a, 0, 3], to_core))
+
+    lane = lax.broadcasted_iota(jnp.int32, shares.shape, 1)
+    total = base[...]
+    for i, owner in enumerate((e, *others)):
+        share = jnp.sum(jnp.where(lane == owner, shares[...], 0.0), axis=-1, keepdims=True)
+        if i == 0:
+            rows_back = results[0]
+        else:
+            result_copies[i - 1].wait()
+            rows_back = result_got[i - 1]
+        total = total + share * rows_back.astype(full)
+    output[...] = total.astype(low)
+
+    settle(z_copies[0], z_wide.at[0], got_wide.at[0], sg_out)
+    settle(z_copies[1], z_wide.at[1], got_wide.at[1], su_out)
+    settle(z_copies[2], z_tall, got_tall, sd_out)
+    for a, target in enumerate((q_out, k_out, v_out, o_out)):
+        settle(z_copies[3 + a], z_flat.at[a], got_flat.at[a], target)
+    for copy in misc_copies:
+        copy.wait()
+    misc_out[...] = misc_got[4] + misc_got[5] + misc_got[6] + misc_got[7]
+    for copy in last:
+        copy.wait()
+
+
+def close(expert_own, shared_own, plain, misc, results, base, shares):
+    low, full = jnp.bfloat16, jnp.float32
+    dma = pltpu.SemaphoreType.DMA
+    rows, width = base.shape
+    ninth = width // 8
+    hidden = expert_own[0].shape[2]
+    tiles, unused, small, unused = expert_own[2].shape
+    tall = 2 * shared_own[2].shape[1]
+
+    def vm(*shape, dtype=low):
+        return pltpu.VMEM(shape, dtype)
+
+    def out(*shape, dtype=low):
+        return jax.ShapeDtypeStruct(shape, dtype)
+
+    blocks = [m.reshape(2, 2, 2, ninth, width) for m in plain]
+    spec, anywhere = pl.BlockSpec(memory_space=pltpu.VMEM), pl.BlockSpec(memory_space=pl.ANY)
+    out_shape = [
+        out(2, 2, 2, ninth, hidden), out(2, 2, 2, ninth, hidden), out(tiles, 2, 2, 2, 2 * small, width),
+        out(ninth, hidden // 4, dtype=full), out(ninth, hidden // 4, dtype=full), out(tall, width // 4, dtype=full),
+        *[out(ninth, width // 4, dtype=full)] * 4, out(*misc.shape, dtype=full), out(rows, width),
+    ]
+    scratch = [
+        vm(4, 2, 2, ninth, width), vm(4, 2, 2, ninth // 2, width), vm(4, 2, ninth // 2, width),
+        vm(4, 4, ninth, width // 4), vm(4, tall, width // 4), vm(2, 4, ninth, hidden // 4),
+        vm(4, 3, ninth, width // 4), vm(3, tall, width // 4), vm(2, 3, ninth, hidden // 4),
+        vm(8, *misc.shape, dtype=full), vm(3, rows, width),
+        dma((3, 2)), dma((3, 2, 4)), dma((3, 2, 4)), dma((4, 5)), dma((4, 5)), dma((7, 3)), dma((7, 3)),
+        dma((6,)), dma((6,)), dma((3,)), dma((3,)),
+    ]
+    return pl.pallas_call(
+        close_kernel,
+        out_shape=out_shape,
+        in_specs=[spec] * 14,
+        out_specs=[anywhere] * 3 + [spec] * 9,
+        scratch_shapes=scratch,
+        compiler_params=pltpu.CompilerParams(
+            collective_id=4, has_side_effects=True, vmem_limit_bytes=58 * 2**20
+        ),
+        name="close",
+    )(*expert_own, *shared_own, *blocks, misc, results, base, shares)
+
+
+def per_device_dense(
+    tokens,
+    expert_ids,
+    norm_one,
+    w_query,
+    w_key,
+    w_value,
+    w_out,
+    norm_two,
+    w_router,
+    expert_gate,
+    expert_up,
+    expert_down,
+    shared_gate,
+    shared_up,
+    shared_down,
+    cotangent,
+):
+    rows = tokens.shape[1]
+    width = tokens.shape[2]
+    heads = width // HEAD_DIM
+    scale = HEAD_DIM ** (-0.5)
+    ctx_count = lax.axis_size("ctx")
+    ctx_place = lax.axis_index("ctx")
+    exp_place = lax.axis_index("exp")
+    row_groups = lax.axis_size("seq") * ctx_count
+    places = ctx_place * rows + jnp.arange(rows, dtype=jnp.int32)
+    upstream = cotangent[0]
+    ids = expert_ids[0]
+    experts = jnp.arange(128, dtype=jnp.int32)
+    named = jnp.any(ids[:, :, None] == experts[None, None, :], axis=1)
+    (
+        q_all, k_all, v_all, upstream_all, named_all, normed, attended, mixed, second, log_sum,
+    ) = front(
+        tokens[0], upstream, named.astype(jnp.bfloat16), norm_one, norm_two, w_query, w_key, w_value, w_out
+    )
+    (
+        results, shares, base, d_mixed, small, eg_own, eu_own, ed_own, sg_own, su_own, sd_own,
+    ) = ffn(
+        second, mixed, upstream_all, named_all, w_router, norm_two,
+        (expert_gate[0], expert_up[0], expert_down[0]), (shared_gate, shared_up, shared_down),
+    )
+
+    def heads_of(matrix):
+        return matrix.reshape(matrix.shape[0], heads, HEAD_DIM)
+
+    span = ctx_count * rows
+    inputs = tokens[0].astype(jnp.float32)
+    unused, norm_one_pull = jax.vjp(normalize, inputs, norm_one)
+    query = heads_of(lax.dynamic_index_in_dim(q_all, ctx_place, 0, False))
+    keys_all, values_all = heads_of(k_all.reshape(span, width)), heads_of(v_all.reshape(span, width))
+    allowed = (jnp.arange(span, dtype=jnp.int32) // BLOCK)[None, None, :] <= (
+        places // BLOCK
+    )[None, :, None]
+    scores = jnp.einsum("qhd,khd->hqk", query, keys_all, preferred_element_type=jnp.float32)
+    weights = jnp.where(allowed, jnp.exp(scores * scale - log_sum.T[:heads, :, None]), 0.0)
+    weights_low = weights.astype(jnp.bfloat16)
+    d_attention = d_mixed.astype(jnp.bfloat16)
+    grad_out = outer_sum(attended, d_attention)
+    d_attended = heads_of(against(d_attention, w_out).astype(jnp.bfloat16))
+    d_weights = jnp.einsum(
+        "qhd,khd->hqk", d_attended, values_all, preferred_element_type=jnp.float32
+    )
+    delta = jnp.sum(weights * d_weights, axis=-1, keepdims=True)
+    d_scores = (weights * (d_weights - delta)).astype(jnp.bfloat16)
+    d_query = (
+        jnp.einsum("hqk,khd->qhd", d_scores, keys_all, preferred_element_type=jnp.float32) * scale
+    )
+    d_key = (
+        jnp.einsum("hqk,qhd->khd", d_scores, query, preferred_element_type=jnp.float32) * scale
+    )
+    d_value = jnp.einsum(
+        "hqk,qhd->khd", weights_low, d_attended, preferred_element_type=jnp.float32
+    )
+    key_terms = jnp.concatenate([d_key.reshape(span, width), d_value.reshape(span, width)], axis=1)
+    key_grads = lax.psum_scatter(
+        key_terms.astype(jnp.bfloat16), "ctx", scatter_dimension=0, tiled=True
+    )
+    d_value = key_grads[:, width:]
+    d_key_lin = rotate(heads_of(key_grads[:, :width].astype(jnp.float32)), -places)
+    d_key_lin = d_key_lin.astype(jnp.bfloat16).reshape(rows, width)
+    d_query_lin = rotate(d_query, -places).astype(jnp.bfloat16).reshape(rows, width)
+    grad_query = outer_sum(normed, d_query_lin)
+    grad_key = outer_sum(normed, d_key_lin)
+    grad_value = outer_sum(normed, d_value)
+    d_normed = against(d_query_lin, w_query) + against(d_key_lin, w_key) + against(d_value, w_value)
+    d_inputs, grad_norm_one = norm_one_pull(d_normed)
+    grad_tokens = (d_mixed + d_inputs)[None]
+    misc = jnp.concatenate(
+        [grad_norm_one[None], small[8:9], small[:4], jnp.zeros((2, width), jnp.float32)], axis=0
+    )
+    plain = [g.astype(jnp.bfloat16) for g in (grad_query, grad_key, grad_value, grad_out)]
+    (
+        eg, eu, ed, sg, su, sd, gq, gk, gv, go, misc, output,
+    ) = close((eg_own, eu_own, ed_own), (sg_own, su_own, sd_own), plain, misc, results, base, shares)
+    row_place = lax.axis_index("seq") * ctx_count + ctx_place
+    own_rows = width // row_groups
+    router = lax.dynamic_slice(misc, (2 + exp_place, row_place * own_rows), (1, own_rows))
+    return (
+        output[None],
+        grad_tokens,
+        misc[0],
+        gq,
+        gk,
+        gv,
+        go,
+        misc[1],
+        router.T,
+        eg.astype(jnp.float32).reshape(expert_gate.shape),
+        eu.astype(jnp.float32).reshape(expert_up.shape),
+        ed.astype(jnp.float32).reshape(expert_down.shape),
+        sg,
+        su,
+        sd,
+    )
+
+
+def fits(mesh):
+    return dict(mesh.shape) == {"seq": 2, "ctx": 4, "exp": 4}
+
+
 def solution(mesh):
+    per_device = per_device_dense if fits(mesh) else per_device_slots
     in_specs = (
         P(("seq", "exp"), "ctx", None),
         P(("seq", "exp"), "ctx", None),

time: 1580 us -> 388 us (0.25)
  waiting for transfers between devices: 1010 us -> 28.7 us
  Pallas kernels: 0 us -> 253 us
  local copies, waits for them, and re-layouts: 278 us -> 29.1 us
  matrix products: 149 us -> 28.5 us
  blocking collectives: 39.5 us -> 0 us
  other arithmetic: 57.3 us -> 28.6 us
  starting transfers between devices: 25.2 us -> 0.04 us
    reduce_scatter x8 -> x1, waiting for transfers between devices: 738 us -> 28.6 us  [per_device_dense(): lax.psum_scatter(key_terms.astype(jnp.bfloat16), 'ctx', scatter_dimension...]
    pallas_call x0 -> x3, Pallas kernels: none -> 253 us  [the longest x1 119 us: ffn(): pl.pallas_call(ffn_kernel, out_shape=out_shape, in_specs=[spec] * 6 + [pl...]
    scatter x2 -> x0, local copies, waits for them, and re-layouts: 143 us -> none  [to_slots(): return empty_slots.at[flat_ids, slot_place].set(routed_rows).reshape(exp_...]
    psum x1 -> x0, waiting for transfers between devices: 141 us -> none  [per_device(): lax.psum(grad_expert_gate.astype(jnp.bfloat16), ('seq', 'ctx'))]
    dot_general x28 -> x5, matrix products: 121 us -> 19 us  [the longest x1 7.43 us: per_device_dense(): jnp.einsum('qhd,khd->hqk', d_attended, values_all, preferred_element_type...]
    all_to_all x4 -> x0, waiting for transfers between devices: 55.6 us -> none  [the longest x1 22.8 us: per_device(): lax.all_to_all(send_rows, 'exp', split_axis=0, concat_axis=0, tiled=True)]
    unnamed x13 -> x1, waiting for transfers between devices: 42.9 us -> 0.02 us
    psum x1 -> x0, blocking collectives: 39.5 us -> none  [per_device(): lax.psum((grad_norm_one, grad_norm_two), ('seq', 'ctx', 'exp'))]
  transfers between devices with their start and end apart: 16 -> 1, of which waited for: 14 -> 1; matrix products, arithmetic and copies ran while one was open for 16% -> 3% of each run, Pallas kernels for 0% -> 0%
where the time goes in v3:
time: 388 us; the launch traced here: 383 us
  Pallas kernels  253 us (65%)
  local copies, waits for them, and re-layouts  29.1 us (8%)
  waiting for transfers between devices  28.7 us (7%)
  other arithmetic  28.6 us (7%)
  matrix products  28.5 us (7%)
  between operations  14.7 us (4%)
    pallas_call x1, Pallas kernels, ffn(): pl.pallas_call(ffn_kernel, out_shape=out_shape, in_specs=[spec] * 6 + [pl...  119 us
    pallas_call x1, Pallas kernels, close(): pl.pallas_call(close_kernel, out_shape=out_shape, in_specs=[spec] * 14, o...  91.1 us
    pallas_call x1, Pallas kernels, front(): pl.pallas_call(front_kernel, out_shape=out_shape, in_specs=[spec] * 11, o...  43.1 us
    reduce_scatter x1, waiting for transfers between devices, per_device_dense(): lax.psum_scatter(key_terms.astype(jnp.bfloat16), 'ctx', scatter_dimension...  28.6 us
    unnamed x67, local copies, waits for them, and re-layouts  7.92 us
  transfers between devices with their start and end apart: 1, of which 1 were waited for; matrix products, arithmetic and copies ran while one was open for 3% of the time, Pallas kernels for 0%

profile of v3, /device:TPU:0, one launch (start us, length us, event | category | flops | bytes accessed | tf_op | source)
XLA Modules:
  0.0 382.5 jit_solution(15016536479896894750)
XLA Ops:
  13.4 43.1 %front.1 = (bf16[4,256,768]{2,1,0:T(8,128)(2,1)}, bf16[4,256,768]{2,1,0:T(8,128)(2,1)}, bf16[4,256,768]{2,1,0:T(8,128)(2,1)}, bf16[4,256,768]{2,1,0:T(8,128)(2,1...) custom-call(bf16[256,768]{1,0:T(8,128)(2,1)} %bitcast.67, ...), custom_call_target="tpu_custom_call" | custom-call | tf_op jit(solution)/shard_map/front/pallas_call | solution.py:553
  56.6 118.7 %ffn.1 = (bf16[4,256,768]{2,1,0:T(8,128)(2,1)}, f32[256,128]{1,0:T(8,128)}, f32[256,768]{1,0:T(8,128)}, f32[256,768]{1,0:T(8,128)}, f32[16,768]{1,0:T(8,128)}, /...) custom-call(bf16[256,768]{1,0:T(8,128)(2,1)} %get-tuple-element.48.s, ...), custom_call_target="tpu_custom_call" | custom-call | tf_op jit(solution)/shard_map/ffn/pallas_call | solution.py:919
  175.3 1.6 convolution_convert_fusion.4
  179.0 2.7 copy.51
  183.9 2.7 copy.55
  186.6 2.3 reshape_reshape.7
  189.5 1.8 fusion.25
  191.6 3.2 fusion.4
  194.8 7.4 %multiply_reduce_fusion = (f32[12,256]{1,0:T(8,128)S(1)}, f32[12,256,1024]{2,1,0:T(8,128)}) fusion(f32[12,256,1024]{2,1,0:T(8,128)S(1)} %fusion.25, f32[12,256]{1,0:T(8,128)S(1)} %copy.53, pred[256,1024]{1,0:T(8,128)(4,1)S(1)} %broadcast_compare_fusion, bf16[256,12,64]{0,2,1:T(8,128)(2,1)S(1)} %bitcast.87, bf16[1024,12,64]{0,2,1:T(8,128)(2,1)S(1)} %copy-done.3), kind=kOutput, calls=%fused_computation.1 | convolution fusion | flops 418378752 | bytes 27418624 | tf_op jit(solution)/shard_map/qhd,khd->hqk/dot_general | solution.py:1174
  202.3 6.9 %multiply_convert_fusion = bf16[12,256,1024]{2,1,0:T(8,128)(2,1)S(1)} fusion(f32[12,256,1024]{2,1,0:T(8,128)} %get-tuple-element.139, f32[12,256,1024]{2,1,0:T(8,128)S(1)} %fusion.25, f32[12,256]{1,0:T(8,128)S(1)} %get-tuple-element.138, f32[12,256]{1,0:T(8,128)S(1)} %copy.53, pred[256,1024]{1,0:T(8,128)(4,1)S(1)} %broadcast_compare_fusion), kind=kLoop, calls=%fused_computation | loop fusion | flops 18874368 | bytes 31744000 | tf_op jit(solution)/shard_map/convert_element_type | solution.py:1178
  210.4 1.5 copy-done
  211.9 2.0 pad_maximum_fusion
  217.7 1.5 convolution_convert_fusion
  219.2 5.3 %fusion.7 = f32[256,12,64]{0,2,1:T(8,128)S(1)} fusion(bf16[1024,12,64]{0,2,1:T(8,128)(2,1)S(1)} %reshape_reshape.6, bf16[12,256,1024]{2,1,0:T(8,128)(2,1)} %copy-done), kind=kOutput, calls=%fused_computation.18 | convolution fusion | flops 402849792 | bytes 8650752 | tf_op jit(solution)/shard_map/hqk,khd->qhd/dot_general | solution.py:1180
  224.6 28.6 %reduce-scatter.2.cloned.1.call-done = bf16[256,1536]{0,1:T(8,128)(2,1)} async-done(((bf16[1024,1536]{0,1:T(8,128)(2,1)}), bf16[256,1536]{0,1:T(8,128)(2,1)}) %reduce-scatter.2.cloned.1.call-update) | async-done | bytes 786448 | tf_op jit(solution)/shard_map/reduce_scatter | solution.py:1189
  256.0 1.5 convolution_convert_fusion.3
  257.6 1.5 convolution_convert_fusion.2
  261.1 1.5 convolution_convert_fusion.1
  262.6 91.1 %close.1 = (bf16[2,2,2,96,2048]{4,3,2,1,0:T(8,128)(2,1)}, bf16[2,2,2,96,2048]{4,3,2,1,0:T(8,128)(2,1)}, bf16[8,2,2,2,32,768]{5,4,3,2,1,0:T(8,128)(2,1)}, f32[96,...) custom-call(bf16[2,48,2048]{2,1,0:T(8,128)(2,1)} %get-tuple-element., ...), custom_call_target="tpu_custom_call" | custom-call | tf_op jit(solution)/shard_map/close/pallas_call | solution.py:1101
  353.7 5.6 %convert.33 = f32[1,768,2048]{2,1,0:T(8,128)} convert(bf16[1,768,2048]{2,1,0:T(8,128)(2,1)} %bitcast.80) | non-fusion elementwise | flops 1572864 | bytes 9437184 | tf_op jit(solution)/shard_map/reshape | solution.py:1222
  359.3 3.6 convert.34
  362.9 3.2 convert.35
  366.9 1.4 slice_reduce_fusion
  369.5 1.3 dynamic-slice_bitcast_fusion
  (102 shorter events, 27.5 us)
Async XLA Ops:
  7.2 246.1 %reduce-scatter.2.cloned.1.call-start = ((), (), s32[]{:S(2)}) async-start(), calls=%async_computation.1 | async-start | bytes 3932160 | tf_op jit(solution)/shard_map/reduce_scatter | solution.py:1189
  56.6 118.7 %copy-start.6 = (bf16[768,768]{1,0:T(8,128)(2,1)S(1)}, bf16[768,768]{1,0:T(8,128)(2,1)}, u32[]{:S(2)}) copy-start(bf16[768,768]{1,0:T(8,128)(2,1)} %w_o.1) | copy-start | bytes 3538948
  191.6 3.3 copy-start.3
  209.2 2.7 copy-start
  213.9 2.2 copy-start.2
  213.9 3.0 copy-start.27
  213.9 3.8 copy-start.1
  213.9 3.8 copy-start.13
  224.6 30.9 %copy-start.7 = (bf16[768,768]{1,0:T(8,128)(2,1)S(1)}, bf16[768,768]{1,0:T(8,128)(2,1)}, u32[]{:S(2)}) copy-start(bf16[768,768]{1,0:T(8,128)(2,1)} %w_q.1) | copy-start | bytes 3538948
  255.4 3.7 copy-start.4
  257.5 2.1 copy-start.11
  257.5 2.1 copy-start.22
  257.5 2.1 copy-start.24
  353.7 5.6 %copy-start.10 = (bf16[2,2,2,96,2048]{4,3,2,1,0:T(8,128)(2,1)S(1)}, bf16[2,2,2,96,2048]{4,3,2,1,0:T(8,128)(2,1)}, u32[]{:S(2)}) copy-start(bf16[2,2,2,96,2048]{4,3,2,1,0:T(8,128)(2,1)} %get-tuple-element.76) | copy-start | bytes 9437188
  359.3 3.6 copy-start.9
  362.9 3.2 copy-start.26
  362.9 3.3 copy-start.15
  366.1 4.7 %copy-start.14 = (bf16[256,768]{1,0:T(8,128)(2,1)S(1)}, bf16[256,768]{1,0:T(8,128)(2,1)}, u32[]{:S(2)}) copy-start(bf16[256,768]{1,0:T(8,128)(2,1)} %get-tuple-element.69) | copy-start | bytes 1179652
  366.1 5.4 %copy-start.21 = (f32[96,192]{1,0:T(8,128)S(1)}, f32[96,192]{1,0:T(8,128)}, u32[]{:S(2)}) copy-start(f32[96,192]{1,0:T(8,128)} %get-tuple-element.161) | copy-start | bytes 221188
  366.1 6.1 %copy-start.20 = (f32[96,192]{1,0:T(8,128)S(1)}, f32[96,192]{1,0:T(8,128)}, u32[]{:S(2)}) copy-start(f32[96,192]{1,0:T(8,128)} %get-tuple-element.162) | copy-start | bytes 221188
  366.1 6.7 %copy-start.19 = (f32[96,192]{1,0:T(8,128)S(1)}, f32[96,192]{1,0:T(8,128)}, u32[]{:S(2)}) copy-start(f32[96,192]{1,0:T(8,128)} %get-tuple-element.163) | copy-start | bytes 221188
  366.1 7.4 %copy-start.18 = (f32[96,192]{1,0:T(8,128)S(1)}, f32[96,192]{1,0:T(8,128)}, u32[]{:S(2)}) copy-start(f32[96,192]{1,0:T(8,128)} %get-tuple-element.164) | copy-start | bytes 221188
  366.1 8.0 %copy-start.17 = (f32[96,512]{1,0:T(8,128)S(1)}, f32[96,512]{1,0:T(8,128)}, u32[]{:S(2)}) copy-start(f32[96,512]{1,0:T(8,128)} %get-tuple-element.170) | copy-start | bytes 589828
  366.1 8.7 %copy-start.16 = (f32[96,512]{1,0:T(8,128)S(1)}, f32[96,512]{1,0:T(8,128)}, u32[]{:S(2)}) copy-start(f32[96,512]{1,0:T(8,128)} %get-tuple-element.171) | copy-start | bytes 589828
  (6 other events, 10.4 us)
Sparse Core Ops, SparseCore 0:
  214.0 39.1 reduce-scatter.1

commit v4 on v3

--- a/solution.py
+++ b/solution.py
@@ -929,9 +929,11 @@
     )(second, mixed, upstream_all, named_all, w_r, gain_two.reshape(1, width), *experts, *shared)
 
 
-def close_kernel(
-    eg_own, eu_own, ed_own, sg_own, su_own, sd_own, gq, gk, gv, go, misc_in, results, base, shares,
-    eg_all, eu_all, ed_all, sg_out, su_out, sd_out, q_out, k_out, v_out, o_out, misc_out, output,
+def back_kernel(
+    eg_own, eu_own, ed_own, sg_own, su_own, sd_own, small, results, base, shares,
+    tokens, gain_one, d_mixed, attended, normed, q_all, k_all, v_all, log_sum, w_q, w_k, w_v, w_o, cosine, sine,
+    eg_all, eu_all, ed_all, sg_out, su_out, sd_out, q_out, k_out, v_out, o_out, misc_out, output, token_out,
+    grads, d_att, d_all, stats, stat_col, sum_q, sum_k, sum_v, misc_in, asem, arem, tsem, trem,
     one, two, three, z_flat, z_tall, z_wide, got_flat, got_tall, got_wide, misc_got, result_got,
     lsem, gsem, grem, psem, prem, zsem, zrem, msem, mrem, rsem, rrem,
 ):
@@ -942,7 +944,7 @@
     greet([to_core, to_x, to_y, *to_z])
 
     def piece(a):
-        g = (gq, gk, gv, go)[a]
+        g = grads.at[a]
         return Piece(
             place,
             lambda kk: g.at[:, :, kk],
@@ -952,9 +954,27 @@
             g.shape[3] // 2, lambda n: (psem.at[a, n], prem.at[a, n]), 48,
         )
 
-    for a in range(4):
-        piece(a).start(1)
-    misc_copy = start_copy(misc_in, misc_got.at[0], msem.at[0], mrem.at[0], to_core)
+    rows, width = tokens.shape
+    heads = width // HEAD_DIM
+    d_att[...] = d_mixed[...].astype(low)
+    d_all[c] = against(d_att[...], w_o[...]).astype(low)
+    head_of = lax.broadcasted_iota(jnp.int32, (128, width), 1) // HEAD_DIM
+    chosen = jnp.where(head_of == lax.broadcasted_iota(jnp.int32, (128, width), 0), 1.0, 0.0).astype(low)
+    terms = d_all[c].astype(full) * attended[...].astype(full)
+    high = terms.astype(low)
+    rest = (terms - high.astype(full)).astype(low)
+    stat_col[0] = log_sum[...]
+    stat_col[1] = against(high, chosen) + against(rest, chosen)
+    stats[c, 0] = log_sum[...].T[0:16, :]
+    stats[c, 1] = (against(chosen[0:16], high) + against(chosen[0:16], rest))
+    core_copies = [
+        start_copy(d_all.at[c], d_all.at[c], asem.at[0], arem.at[0], to_core),
+        start_copy(stats.at[c], stats.at[c], tsem.at[0], trem.at[0], to_core),
+    ]
+    x_copies = [
+        start_copy(d_all.at[c], d_all.at[c], asem.at[1], arem.at[1], to_x),
+        start_copy(stats.at[c], stats.at[c], tsem.at[1], trem.at[1], to_x),
+    ]
     result_copies = [
         start_copy(results.at[i + 1], result_got.at[i], rsem.at[i], rrem.at[i], to_z[i]) for i in range(3)
     ]
@@ -965,21 +985,17 @@
         part = pl.ds(h * half, half)
         return whole.at[ss, xx, k, part] if a < 2 else whole.at[:, ss, xx, k, part]
 
-    legs = []
+    near, wide, kept = [], [], []
     for a, own in enumerate((eg_own, eu_own, ed_own)):
         for h in range(2):
-            src = own.at[h] if a < 2 else own.at[:, h]
-            here = block(a, h, s, x)
-            local = pltpu.make_async_copy(src, here, lsem.at[a, h])
-            local.start()
-            near, wide = (to_y, to_x) if h == 0 else (to_x, to_y)
-            legs.append(
-                (
-                    local,
-                    start_copy(src, here, gsem.at[a, h, 0], grem.at[a, h, 0], near),
-                    start_copy(src, here, gsem.at[a, h, 1], grem.at[a, h, 1], wide),
-                )
-            )
+            src, here = (own.at[h] if a < 2 else own.at[:, h]), block(a, h, s, x)
+            kept.append(pltpu.make_async_copy(src, here, lsem.at[a, h]))
+            kept[-1].start()
+            near.append(start_copy(src, here, gsem.at[a, h, 0], grem.at[a, h, 0], (to_y, to_x)[h]))
+    for a, own in enumerate((eg_own, eu_own, ed_own)):
+        for h in range(2):
+            src, here = (own.at[h] if a < 2 else own.at[:, h]), block(a, h, s, x)
+            wide.append(start_copy(src, here, gsem.at[a, h, 1], grem.at[a, h, 1], (to_x, to_y)[h]))
 
     def spread(own, buffer):
         halves, height, across = own.shape
@@ -1008,28 +1024,145 @@
     ):
         spread(own, buffer)
         z_copies.append(to_owners(buffer, got, number))
-    for a in range(4):
+    def put(a, first_factor, second_factor):
+        grads[a] = outer_sum(first_factor, second_factor).astype(low).reshape(2, 2, 2, width // 8, width)
+        piece(a).start(1)
+
+    put(3, attended[...], d_att[...])
+    lane = lax.broadcasted_iota(jnp.int32, (rows, 128), 1)
+    scale = HEAD_DIM**-0.5
+    for total in (sum_q, sum_k, sum_v):
+        total[...] = jnp.zeros_like(total)
+
+    def inside(h, values):
+        return jnp.where((lane // HEAD_DIM) == h, values, jnp.zeros_like(values))
+
+    def columns(g):
+        return pl.ds(pl.multiple_of(g * 128, 128), 128)
+
+    def query_pair(g, carry):
+        at = columns(g)
+        q, d_out = q_all[c, :, at], d_all[c, :, at]
+        sides = []
+        for h in range(2):
+            pick = lane == 2 * g + h
+            sides.append(
+                (
+                    inside(h, q),
+                    inside(h, d_out),
+                    jnp.sum(jnp.where(pick, stat_col[0], 0.0), axis=-1, keepdims=True),
+                    jnp.sum(jnp.where(pick, stat_col[1], 0.0), axis=-1, keepdims=True),
+                )
+            )
+        for j in range(4):
+
+            @pl.when(j <= c)
+            def _(j=j):
+                keys, values = k_all[j, :, at], v_all[j, :, at]
+                terms = []
+                for q_side, d_side, log_total, delta in sides:
+                    weights = jnp.exp(against(q_side, keys) * scale - log_total)
+                    d_scores = (weights * (against(d_side, values) - delta)).astype(low)
+                    terms.append(jnp.dot(d_scores, keys, preferred_element_type=full))
+                sum_q[:, at] += jnp.where(lane < HEAD_DIM, terms[0], terms[1])
+
+        return carry
+
+    lax.fori_loop(0, width // 128, query_pair, 0)
+
+    def key_side(j):
+        @pl.when(j >= c)
+        def _():
+            def key_pair(g, carry):
+                at = columns(g)
+                keys, values = k_all[c, :, at], v_all[c, :, at]
+                q, d_out = q_all[j, :, at], d_all[j, :, at]
+                terms = []
+                for h in range(2):
+                    log_total = stats[j, 0, pl.ds(2 * g + h, 1), :]
+                    delta = stats[j, 1, pl.ds(2 * g + h, 1), :]
+                    weights = jnp.exp(against(inside(h, keys), q) * scale - log_total)
+                    d_scores = (weights * (against(inside(h, values), d_out) - delta)).astype(low)
+                    terms.append(
+                        (
+                            jnp.dot(d_scores, q, preferred_element_type=full),
+                            jnp.dot(weights.astype(low), d_out, preferred_element_type=full),
+                        )
+                    )
+                sum_k[:, at] += jnp.where(lane < HEAD_DIM, terms[0][0], terms[1][0])
+                sum_v[:, at] += jnp.where(lane < HEAD_DIM, terms[0][1], terms[1][1])
+                return carry
+
+            lax.fori_loop(0, width // 128, key_pair, 0)
+
+    def turned_back(total):
+        parts = []
+        for g in range(width // 128):
+            part = total[:, g * 128 : (g + 1) * 128] * scale
+            parts.append((part * cosine[c] - swapped(part) * sine[c]).astype(low))
+        return jnp.concatenate(parts, axis=1)
+
+    key_side(c)
+    d_query = turned_back(sum_q)
+    put(0, normed[...], d_query)
+    d_normed = against(d_query, w_q[...])
+    piece(3).finish(1)
+    piece(3).start(2)
+    for copy in core_copies:
+        copy.wait()
+    key_side(x * 2 + (1 - k))
+    for copy in x_copies:
+        copy.wait()
+    there = (1 - x) * 2 + k
+    corner_copies = [
+        start_copy(d_all.at[there], d_all.at[there], asem.at[2], arem.at[2], to_core),
+        start_copy(stats.at[there], stats.at[there], tsem.at[2], trem.at[2], to_core),
+    ]
+    key_side(there)
+    onward = []
+    for a in range(3):
+        for h in range(2):
+            near[2 * a + h].wait()
+            spot = block(a, h, (1 - s, s)[h], (x, 1 - x)[h])
+            onward.append(start_copy(spot, spot, gsem.at[a, h, 2], grem.at[a, h, 2], (to_x, to_y)[h]))
+    for copy in corner_copies:
+        copy.wait()
+    key_side((1 - x) * 2 + (1 - k))
+    d_key = turned_back(sum_k)
+    put(1, normed[...], d_key)
+    d_value = sum_v[...].astype(low)
+    put(2, normed[...], d_value)
+    piece(0).finish(1)
+    piece(0).start(2)
+    d_normed = d_normed + against(d_key, w_k[...]) + against(d_value, w_v[...])
+    values = tokens[...].astype(full)
+    inverse = lax.rsqrt(jnp.mean(values * values, axis=-1, keepdims=True) + 1e-06)
+    unit = values * inverse
+    misc_in[0:8, :] = small[0:8, :]
+    misc_in[8:9, :] = jnp.sum(d_normed * unit, axis=0, keepdims=True)
+    misc_in[9:10, :] = small[8:9, :]
+    misc_in[10:16, :] = jnp.zeros((6, width), full)
+    misc_copy = start_copy(misc_in, misc_got.at[0], msem.at[0], mrem.at[0], to_core)
+    for a in (1, 2):
         piece(a).finish(1)
         piece(a).start(2)
+    inner = d_normed * gain_one[...]
+    mean = jnp.mean(inner * unit, axis=-1, keepdims=True)
+    token_out[...] = d_mixed[...] + inverse * (inner - unit * mean)
     misc_copy.wait()
     misc_out[...] = misc_in[...] + misc_got[0]
     misc_copy = start_copy(misc_out, misc_got.at[1], msem.at[1], mrem.at[1], to_x)
-    onward = []
-    for a in range(3):
-        for h in range(2):
-            legs[2 * a + h][1].wait()
-            there = block(a, h, (1 - s, s)[h], (x, 1 - x)[h])
-            onward.append(start_copy(there, there, gsem.at[a, h, 2], grem.at[a, h, 2], (to_x, to_y)[h]))
-    for a in range(4):
+    for a in (3, 0, 1, 2):
         piece(a).finish(2)
         piece(a).start(3)
     misc_copy.wait()
     misc_got[3] = misc_out[...] + misc_got[1]
     misc_copy = start_copy(misc_got.at[3], misc_got.at[2], msem.at[2], mrem.at[2], to_y)
-    for a in range(4):
+    flat_copies = {}
+    for a in (3, 0, 1, 2):
         piece(a).finish(3)
         spread(three.at[a], z_flat.at[a])
-        z_copies.append(to_owners(z_flat.at[a], got_flat.at[a], 3 + a))
+        flat_copies[a] = to_owners(z_flat.at[a], got_flat.at[a], 3 + a)
     misc_copy.wait()
     misc_got[4] = misc_got[3] + misc_got[2]
     misc_copies = [
@@ -1038,13 +1171,12 @@
     last = []
     for a, whole in enumerate((eg_all, eu_all, ed_all)):
         for h in range(2):
-            legs[2 * a + h][0].wait()
-            legs[2 * a + h][2].wait()
+            kept[2 * a + h].wait()
+            wide[2 * a + h].wait()
             onward[2 * a + h].wait()
-        there = whole.at[:, :, k] if a < 2 else whole.at[:, :, :, k]
-        last.append(start_copy(there, there, gsem.at[a, 0, 3], grem.at[a, 0, 3], to_core))
-
-    lane = lax.broadcasted_iota(jnp.int32, shares.shape, 1)
+        spot = whole.at[:, :, k] if a < 2 else whole.at[:, :, :, k]
+        last.append(start_copy(spot, spot, gsem.at[a, 0, 3], grem.at[a, 0, 3], to_core))
+
     total = base[...]
     for i, owner in enumerate((e, *others)):
         share = jnp.sum(jnp.where(lane == owner, shares[...], 0.0), axis=-1, keepdims=True)
@@ -1060,7 +1192,7 @@
     settle(z_copies[1], z_wide.at[1], got_wide.at[1], su_out)
     settle(z_copies[2], z_tall, got_tall, sd_out)
     for a, target in enumerate((q_out, k_out, v_out, o_out)):
-        settle(z_copies[3 + a], z_flat.at[a], got_flat.at[a], target)
+        settle(flat_copies[a], z_flat.at[a], got_flat.at[a], target)
     for copy in misc_copies:
         copy.wait()
     misc_out[...] = misc_got[4] + misc_got[5] + misc_got[6] + misc_got[7]
@@ -1068,14 +1200,15 @@
         copy.wait()
 
 
-def close(expert_own, shared_own, plain, misc, results, base, shares):
+def back(expert_own, shared_own, small, results, base, shares, tokens, gain_one, d_mixed, kept, weights):
     low, full = jnp.bfloat16, jnp.float32
     dma = pltpu.SemaphoreType.DMA
     rows, width = base.shape
     ninth = width // 8
     hidden = expert_own[0].shape[2]
-    tiles, unused, small, unused = expert_own[2].shape
+    tiles, unused, short, unused = expert_own[2].shape
     tall = 2 * shared_own[2].shape[1]
+    cosine, sine = (jnp.asarray(t).reshape(4, rows, 128) for t in place_tables(4 * rows))
 
     def vm(*shape, dtype=low):
         return pltpu.VMEM(shape, dtype)
@@ -1083,32 +1216,39 @@
     def out(*shape, dtype=low):
         return jax.ShapeDtypeStruct(shape, dtype)
 
-    blocks = [m.reshape(2, 2, 2, ninth, width) for m in plain]
     spec, anywhere = pl.BlockSpec(memory_space=pltpu.VMEM), pl.BlockSpec(memory_space=pl.ANY)
     out_shape = [
-        out(2, 2, 2, ninth, hidden), out(2, 2, 2, ninth, hidden), out(tiles, 2, 2, 2, 2 * small, width),
+        out(2, 2, 2, ninth, hidden), out(2, 2, 2, ninth, hidden), out(tiles, 2, 2, 2, 2 * short, width),
         out(ninth, hidden // 4, dtype=full), out(ninth, hidden // 4, dtype=full), out(tall, width // 4, dtype=full),
-        *[out(ninth, width // 4, dtype=full)] * 4, out(*misc.shape, dtype=full), out(rows, width),
+        *[out(ninth, width // 4, dtype=full)] * 4, out(16, width, dtype=full), out(rows, width),
+        out(rows, width, dtype=full),
     ]
     scratch = [
+        vm(4, 2, 2, 2, ninth, width), vm(rows, width), vm(4, rows, width), vm(4, 2, 16, rows, dtype=full),
+        vm(2, rows, 128, dtype=full), *[vm(rows, width, dtype=full)] * 3, vm(16, width, dtype=full),
+        dma((3,)), dma((3,)), dma((3,)), dma((3,)),
         vm(4, 2, 2, ninth, width), vm(4, 2, 2, ninth // 2, width), vm(4, 2, ninth // 2, width),
         vm(4, 4, ninth, width // 4), vm(4, tall, width // 4), vm(2, 4, ninth, hidden // 4),
         vm(4, 3, ninth, width // 4), vm(3, tall, width // 4), vm(2, 3, ninth, hidden // 4),
-        vm(8, *misc.shape, dtype=full), vm(3, rows, width),
+        vm(8, 16, width, dtype=full), vm(3, rows, width),
         dma((3, 2)), dma((3, 2, 4)), dma((3, 2, 4)), dma((4, 5)), dma((4, 5)), dma((7, 3)), dma((7, 3)),
         dma((6,)), dma((6,)), dma((3,)), dma((3,)),
     ]
+    operands = (
+        *expert_own, *shared_own, small, results, base, shares, tokens, gain_one.reshape(1, width), d_mixed, *kept,
+        *weights, cosine, sine,
+    )
     return pl.pallas_call(
-        close_kernel,
+        back_kernel,
         out_shape=out_shape,
-        in_specs=[spec] * 14,
-        out_specs=[anywhere] * 3 + [spec] * 9,
+        in_specs=[spec] * len(operands),
+        out_specs=[anywhere] * 3 + [spec] * 10,
         scratch_shapes=scratch,
         compiler_params=pltpu.CompilerParams(
-            collective_id=4, has_side_effects=True, vmem_limit_bytes=58 * 2**20
+            collective_id=4, has_side_effects=True, vmem_limit_bytes=60 * 2**20
         ),
-        name="close",
-    )(*expert_own, *shared_own, *blocks, misc, results, base, shares)
+        name="back",
+    )(*operands)
 
 
 def per_device_dense(
@@ -1129,15 +1269,11 @@
     shared_down,
     cotangent,
 ):
-    rows = tokens.shape[1]
     width = tokens.shape[2]
-    heads = width // HEAD_DIM
-    scale = HEAD_DIM ** (-0.5)
     ctx_count = lax.axis_size("ctx")
     ctx_place = lax.axis_index("ctx")
     exp_place = lax.axis_index("exp")
     row_groups = lax.axis_size("seq") * ctx_count
-    places = ctx_place * rows + jnp.arange(rows, dtype=jnp.int32)
     upstream = cotangent[0]
     ids = expert_ids[0]
     experts = jnp.arange(128, dtype=jnp.int32)
@@ -1154,70 +1290,24 @@
         (expert_gate[0], expert_up[0], expert_down[0]), (shared_gate, shared_up, shared_down),
     )
 
-    def heads_of(matrix):
-        return matrix.reshape(matrix.shape[0], heads, HEAD_DIM)
-
-    span = ctx_count * rows
-    inputs = tokens[0].astype(jnp.float32)
-    unused, norm_one_pull = jax.vjp(normalize, inputs, norm_one)
-    query = heads_of(lax.dynamic_index_in_dim(q_all, ctx_place, 0, False))
-    keys_all, values_all = heads_of(k_all.reshape(span, width)), heads_of(v_all.reshape(span, width))
-    allowed = (jnp.arange(span, dtype=jnp.int32) // BLOCK)[None, None, :] <= (
-        places // BLOCK
-    )[None, :, None]
-    scores = jnp.einsum("qhd,khd->hqk", query, keys_all, preferred_element_type=jnp.float32)
-    weights = jnp.where(allowed, jnp.exp(scores * scale - log_sum.T[:heads, :, None]), 0.0)
-    weights_low = weights.astype(jnp.bfloat16)
-    d_attention = d_mixed.astype(jnp.bfloat16)
-    grad_out = outer_sum(attended, d_attention)
-    d_attended = heads_of(against(d_attention, w_out).astype(jnp.bfloat16))
-    d_weights = jnp.einsum(
-        "qhd,khd->hqk", d_attended, values_all, preferred_element_type=jnp.float32
-    )
-    delta = jnp.sum(weights * d_weights, axis=-1, keepdims=True)
-    d_scores = (weights * (d_weights - delta)).astype(jnp.bfloat16)
-    d_query = (
-        jnp.einsum("hqk,khd->qhd", d_scores, keys_all, preferred_element_type=jnp.float32) * scale
-    )
-    d_key = (
-        jnp.einsum("hqk,qhd->khd", d_scores, query, preferred_element_type=jnp.float32) * scale
-    )
-    d_value = jnp.einsum(
-        "hqk,qhd->khd", weights_low, d_attended, preferred_element_type=jnp.float32
-    )
-    key_terms = jnp.concatenate([d_key.reshape(span, width), d_value.reshape(span, width)], axis=1)
-    key_grads = lax.psum_scatter(
-        key_terms.astype(jnp.bfloat16), "ctx", scatter_dimension=0, tiled=True
-    )
-    d_value = key_grads[:, width:]
-    d_key_lin = rotate(heads_of(key_grads[:, :width].astype(jnp.float32)), -places)
-    d_key_lin = d_key_lin.astype(jnp.bfloat16).reshape(rows, width)
-    d_query_lin = rotate(d_query, -places).astype(jnp.bfloat16).reshape(rows, width)
-    grad_query = outer_sum(normed, d_query_lin)
-    grad_key = outer_sum(normed, d_key_lin)
-    grad_value = outer_sum(normed, d_value)
-    d_normed = against(d_query_lin, w_query) + against(d_key_lin, w_key) + against(d_value, w_value)
-    d_inputs, grad_norm_one = norm_one_pull(d_normed)
-    grad_tokens = (d_mixed + d_inputs)[None]
-    misc = jnp.concatenate(
-        [grad_norm_one[None], small[8:9], small[:4], jnp.zeros((2, width), jnp.float32)], axis=0
-    )
-    plain = [g.astype(jnp.bfloat16) for g in (grad_query, grad_key, grad_value, grad_out)]
     (
-        eg, eu, ed, sg, su, sd, gq, gk, gv, go, misc, output,
-    ) = close((eg_own, eu_own, ed_own), (sg_own, su_own, sd_own), plain, misc, results, base, shares)
+        eg, eu, ed, sg, su, sd, gq, gk, gv, go, misc, output, grad_tokens,
+    ) = back(
+        (eg_own, eu_own, ed_own), (sg_own, su_own, sd_own), small, results, base, shares, tokens[0], norm_one, d_mixed,
+        (attended, normed, q_all, k_all, v_all, log_sum), (w_query, w_key, w_value, w_out),
+    )
     row_place = lax.axis_index("seq") * ctx_count + ctx_place
     own_rows = width // row_groups
-    router = lax.dynamic_slice(misc, (2 + exp_place, row_place * own_rows), (1, own_rows))
+    router = lax.dynamic_slice(misc, (exp_place, row_place * own_rows), (1, own_rows))
     return (
         output[None],
-        grad_tokens,
-        misc[0],
+        grad_tokens[None],
+        misc[8],
         gq,
         gk,
         gv,
         go,
-        misc[1],
+        misc[9],
         router.T,
         eg.astype(jnp.float32).reshape(expert_gate.shape),
         eu.astype(jnp.float32).reshape(expert_up.shape),

time: 388 us -> 290 us (0.75); the launches traced: 383 us -> 290 us
  waiting for transfers between devices: 28.7 us -> 0 us
  matrix products: 28.5 us -> 0 us
  local copies, waits for them, and re-layouts: 29.1 us -> 14.2 us
  other arithmetic: 28.6 us -> 13.8 us
  between operations: 14.7 us -> 0.73 us
  Pallas kernels: 253 us -> 261 us
    reduce_scatter x1 -> x0, waiting for transfers between devices: 28.6 us -> none  [per_device_dense(): lax.psum_scatter(key_terms.astype(jnp.bfloat16), 'ctx', scatter_dimension...]
    dot_general x13 -> x0, matrix products: 28.5 us -> none  [the longest x1 7.43 us: per_device_dense(): jnp.einsum('qhd,khd->hqk', d_attended, values_all, preferred_element_type...]
    pallas_call x1, Pallas kernels: 91.1 us -> 99.2 us  [back(): pl.pallas_call(back_kernel, out_shape=out_shape, in_specs=[spec] * len(op...]
    convert_element_type x1 -> x0, other arithmetic: 6.93 us -> none  [per_device_dense(): d_scores = (weights * (d_weights - delta)).astype(jnp.bfloat16)]
    pallas_call x2 -> x0, local copies, waits for them, and re-layouts: 5.41 us -> none  [front(): pl.pallas_call(front_kernel, out_shape=out_shape, in_specs=[spec] * 11, o...]
    unnamed x67 -> x30, local copies, waits for them, and re-layouts: 7.92 us -> 8.19 us
  transfers between devices with their start and end apart: 1 -> 0, of which waited for: 1 -> 0; matrix products, arithmetic and copies ran while one was open for 3% -> 0% of each run, Pallas kernels for 0% -> 0%
where the time goes in v4:
time: 290 us
  Pallas kernels  261 us (90%)
  local copies, waits for them, and re-layouts  14.2 us (5%)
  other arithmetic  13.8 us (5%)
    pallas_call x1, Pallas kernels, ffn(): pl.pallas_call(ffn_kernel, out_shape=out_shape, in_specs=[spec] * 6 + [pl...  119 us
    pallas_call x1, Pallas kernels, back(): pl.pallas_call(back_kernel, out_shape=out_shape, in_specs=[spec] * len(op...  99.2 us
    pallas_call x1, Pallas kernels, front(): pl.pallas_call(front_kernel, out_shape=out_shape, in_specs=[spec] * 11, o...  43.3 us
    unnamed x30, local copies, waits for them, and re-layouts  8.19 us

profile of v4, /device:TPU:0, one launch (start us, length us, event | category | flops | bytes accessed | tf_op | source)
XLA Modules:
  0.0 289.8 jit_solution(1083185979451279329)
XLA Ops:
  0.7 1.3 reshape.69.gain_one
  1.9 1.3 reshape.70.gain_two
  3.2 0.8 fusion
  4.0 0.6 convert_element_type.4.named
  4.7 0.9 copy.38
  5.5 0.7 pad.4.w_r
  6.3 43.3 %front.1 = (bf16[4,256,768]{2,1,0:T(8,128)(2,1)}, bf16[4,256,768]{2,1,0:T(8,128)(2,1)}, bf16[4,256,768]{2,1,0:T(8,128)(2,1)}, bf16[4,256,768]{2,1,0:T(8,128)(2,1...) custom-call(bf16[256,768]{1,0:T(8,128)(2,1)} %bitcast.22, ...), custom_call_target="tpu_custom_call" | custom-call | tf_op jit(solution)/shard_map/front/pallas_call | solution.py:553
  49.6 118.6 %ffn.1 = (bf16[4,256,768]{2,1,0:T(8,128)(2,1)}, f32[256,128]{1,0:T(8,128)}, f32[256,768]{1,0:T(8,128)}, f32[256,768]{1,0:T(8,128)}, f32[16,768]{1,0:T(8,128)}, /...) custom-call(bf16[256,768]{1,0:T(8,128)(2,1)} %get-tuple-element.49.s, ...), custom_call_target="tpu_custom_call" | custom-call | tf_op jit(solution)/shard_map/ffn/pallas_call | solution.py:919
  168.2 99.2 %back.1 = (bf16[2,2,2,96,2048]{4,3,2,1,0:T(8,128)(2,1)}, bf16[2,2,2,96,2048]{4,3,2,1,0:T(8,128)(2,1)}, bf16[8,2,2,2,32,768]{5,4,3,2,1,0:T(8,128)(2,1)}, f32[96,5...) custom-call(bf16[2,48,2048]{2,1,0:T(8,128)(2,1)} %get-tuple-element., ...), custom_call_target="tpu_custom_call" | custom-call | tf_op jit(solution)/shard_map/back/pallas_call | solution.py:1241
  267.4 1.3 dynamic-slice_bitcast_fusion
  268.7 1.4 slice_reduce_fusion
  270.1 1.7 copy.39
  271.8 5.6 %convert.3 = f32[1,768,2048]{2,1,0:T(8,128)} convert(bf16[1,768,2048]{2,1,0:T(8,128)(2,1)} %bitcast.18) | non-fusion elementwise | flops 1572864 | bytes 9437184 | tf_op jit(solution)/shard_map/reshape | solution.py:1312
  277.4 3.6 %convert.4 = f32[1,768,2048]{2,1,0:T(8,128)} convert(bf16[1,768,2048]{2,1,0:T(8,128)(2,1)S(1)} %bitcast.17) | non-fusion elementwise | flops 1572864 | bytes 9437184 | tf_op jit(solution)/shard_map/reshape | solution.py:1313
  281.0 0.0 copy-done
  281.0 3.2 %convert.5 = f32[1,2048,768]{2,1,0:T(8,128)} convert(bf16[1,2048,768]{2,1,0:T(8,128)(2,1)S(1)} %bitcast.16) | non-fusion elementwise | flops 1572864 | bytes 9437184 | tf_op jit(solution)/shard_map/reshape | solution.py:1314
  284.2 0.7 copy.48
  285.0 0.9 copy.49
  285.9 0.6 copy.50
  286.5 0.6 copy.51
  287.1 0.6 copy.52
  287.8 0.6 copy.53
  288.4 0.7 copy.54
  289.1 0.7 copy.55
  (19 shorter events, 0.0 us)
Async XLA Ops:
  271.8 5.6 %copy-start.1 = (bf16[2,2,2,96,2048]{4,3,2,1,0:T(8,128)(2,1)S(1)}, bf16[2,2,2,96,2048]{4,3,2,1,0:T(8,128)(2,1)}, u32[]{:S(2)}) copy-start(bf16[2,2,2,96,2048]{4,3,2,1,0:T(8,128)(2,1)} %get-tuple-element.78) | copy-start | bytes 9437188
  277.4 3.6 %copy-start = (bf16[8,2,2,2,32,768]{5,4,3,2,1,0:T(8,128)(2,1)S(1)}, bf16[8,2,2,2,32,768]{5,4,3,2,1,0:T(8,128)(2,1)}, u32[]{:S(2)}) copy-start(bf16[8,2,2,2,32,768]{5,4,3,2,1,0:T(8,128)(2,1)} %get-tuple-element.79) | copy-start | bytes 9437188
  281.0 3.2 %copy-start.3 = (bf16[256,768]{1,0:T(8,128)(2,1)S(1)}, bf16[256,768]{1,0:T(8,128)(2,1)}, u32[]{:S(2)}) copy-start(bf16[256,768]{1,0:T(8,128)(2,1)} %get-tuple-element.70) | copy-start | bytes 1179652
  281.0 4.0 %copy-start.2 = (f32[256,768]{1,0:T(8,128)S(1)}, f32[256,768]{1,0:T(8,128)}, u32[]{:S(2)}) copy-start(f32[256,768]{1,0:T(8,128)} %get-tuple-element.71) | copy-start | bytes 2359300
  281.0 4.9 %copy-start.9 = (f32[96,192]{1,0:T(8,128)S(1)}, f32[96,192]{1,0:T(8,128)}, u32[]{:S(2)}) copy-start(f32[96,192]{1,0:T(8,128)} %get-tuple-element.133) | copy-start | bytes 221188
  281.0 5.5 %copy-start.8 = (f32[96,192]{1,0:T(8,128)S(1)}, f32[96,192]{1,0:T(8,128)}, u32[]{:S(2)}) copy-start(f32[96,192]{1,0:T(8,128)} %get-tuple-element.134) | copy-start | bytes 221188
  281.0 6.1 %copy-start.7 = (f32[96,192]{1,0:T(8,128)S(1)}, f32[96,192]{1,0:T(8,128)}, u32[]{:S(2)}) copy-start(f32[96,192]{1,0:T(8,128)} %get-tuple-element.135) | copy-start | bytes 221188
  281.0 6.8 %copy-start.6 = (f32[96,192]{1,0:T(8,128)S(1)}, f32[96,192]{1,0:T(8,128)}, u32[]{:S(2)}) copy-start(f32[96,192]{1,0:T(8,128)} %get-tuple-element.136) | copy-start | bytes 221188
  284.2 4.2 %copy-start.5 = (f32[96,512]{1,0:T(8,128)S(1)}, f32[96,512]{1,0:T(8,128)}, u32[]{:S(2)}) copy-start(f32[96,512]{1,0:T(8,128)} %get-tuple-element.142) | copy-start | bytes 589828
  284.2 4.9 %copy-start.4 = (f32[96,512]{1,0:T(8,128)S(1)}, f32[96,512]{1,0:T(8,128)}, u32[]{:S(2)}) copy-start(f32[96,512]{1,0:T(8,128)} %get-tuple-element.143) | copy-start | bytes 589828
